TPU v7x, 256 devices: a whole 4x4x8 slice. The times are simulated.
256 devices in a mesh: mem: 32 (over z, x), obs: 8 (over y, core).
Axes of the slice: x: 4, y: 4, z: 8, core: 2. Of those that a mesh axis runs over, the one named last changes fastest.
Arguments:
- members: bfloat16 [2048, 4096], P(('mem', 'obs')), may hold values from -9 to 9
- alphas: int32 [8, 4096], replicated, may hold values from 0 to 3
- obs_inputs: float32 [8, 1024], replicated, may hold values from -1 to 1
- block_ids: int32 [1024], P('obs'), may hold values from 0 to 3
- noise_var: float32 [1024], P('obs'), may hold values from 0.5 to 4
- observed: float32 [1024], P('obs'), may hold values from -18 to 18
- perturb: bfloat16 [2048, 1024], P('mem', 'obs'), may hold values from -6 to 6
Outputs:
- updated: float32 [2048, 4096], P(('mem', 'obs'))
All inputs are finite; a program needn't handle non-finite values.
Results may differ from a plain program's by a relative error of at most 0.0035.
Values may be sent and summed in bfloat16 or wider, within the bound.
A program may use at most 256 MiB of HBM per device.

v0:
```python
import math

import jax
import jax.numpy as jnp
from jax import lax
from jax.sharding import PartitionSpec as P

DEGREE = 3


def merged_2(array, axis, combine):
    everything = jax.tree.map(lambda part: lax.all_gather(part, axis), array)
    first = jax.tree.map(lambda part: part[0], everything)

    def lap(k, so_far):
        return combine(so_far, jax.tree.map(lambda part: part[k], everything))

    return lax.fori_loop(1, lax.axis_size(axis), lap, first)


def hermite_table(points):
    values = [jnp.ones_like(points), points]
    for degree in range(1, DEGREE):
        values.append(points * values[degree] - degree * values[degree - 1])
    return jnp.stack(
        [
            values[term_degree] * (1.0 / math.sqrt(math.factorial(term_degree)))
            for term_degree in range(DEGREE + 1)
        ],
        axis=0,
    )


def basis_rows(alphas, points):
    hermite = hermite_table(points)
    levels = jnp.arange(DEGREE + 1, dtype=jnp.int32)
    product = None
    for dim_index in range(alphas.shape[0]):
        selector = (alphas[dim_index][None, :] == levels[:, None]).astype(jnp.float32)
        picked = lax.dot_general(
            hermite[:, dim_index, :],
            selector,
            (((0,), (0,)), ((), ())),
            precision=lax.Precision.HIGHEST,
            preferred_element_type=jnp.float32,
        )
        product = picked if product is None else product * picked
    return product.astype(jnp.bfloat16)


def combine_moments(left_part, right_part):
    left_count, left_param, left_pred, left_cross, left_gram = left_part
    right_count, right_param, right_pred, right_cross, right_gram = right_part
    count_sum = left_count + right_count
    weight = right_count / count_sum
    product = left_count * right_count / count_sum
    shift_param = right_param - left_param
    shift_pred = right_pred - left_pred
    return (
        count_sum,
        left_param + weight * shift_param,
        left_pred + weight * shift_pred,
        left_cross + right_cross + product * shift_param[:, None] * shift_pred[None, :],
        left_gram + right_gram + product * shift_pred[:, None] * shift_pred[None, :],
    )


def shards(members, alphas, obs_inputs, block_ids, noise_var, observed, perturb):
    tile_obs = block_ids.shape[0]
    gathered = lax.all_gather(members, "obs", axis=0, tiled=True)
    group_rows = gathered.shape[0]
    ensemble = group_rows * lax.axis_size("mem")
    contract_last = (((1,), (1,)), ((), ()))
    contract_first = (((0,), (0,)), ((), ()))
    points = lax.dynamic_slice_in_dim(obs_inputs, lax.axis_index("obs") * tile_obs, tile_obs, 1)
    own_basis = basis_rows(alphas, points)
    own_pred = lax.dot_general(
        members,
        lax.all_gather(own_basis, "obs", axis=0, tiled=True),
        contract_last,
        preferred_element_type=jnp.float32,
    ).astype(jnp.bfloat16)
    predicted = lax.all_to_all(own_pred, "obs", split_axis=1, concat_axis=0, tiled=True)
    sum_param = jnp.sum(gathered, axis=0, dtype=jnp.float32)
    sum_pred = jnp.sum(predicted, axis=0, dtype=jnp.float32)
    raw_cross = lax.dot_general(
        gathered, predicted, contract_first, preferred_element_type=jnp.float32
    )
    raw_gram = lax.dot_general(
        predicted, predicted, contract_first, preferred_element_type=jnp.float32
    )
    local_param = sum_param / group_rows
    local_pred = sum_pred / group_rows
    local_cross = raw_cross - group_rows * local_param[:, None] * local_pred[None, :]
    local_gram = raw_gram - group_rows * local_pred[:, None] * local_pred[None, :]
    counts = jnp.full((1,), float(group_rows), jnp.float32)
    merged = merged_2(
        (counts, local_param, local_pred, local_cross, local_gram), "mem", combine_moments
    )
    cross_cov = merged[3]
    pred_gram = merged[4]
    same_block = block_ids[:, None] == block_ids[None, :]
    system = jnp.where(same_block, pred_gram / (ensemble - 1), 0.0) + jnp.diag(noise_var)
    factor = jnp.linalg.cholesky(system)
    innovation = (
        observed[None, :]
        + jnp.sqrt(noise_var)[None, :] * perturb.astype(jnp.float32)
        - predicted.astype(jnp.float32)
    )
    solved = jax.scipy.linalg.cho_solve((factor, True), innovation.T)
    increment = lax.psum_scatter(
        lax.dot_general(
            solved,
            cross_cov,
            (((0,), (1,)), ((), ())),
            precision=lax.Precision.HIGHEST,
            preferred_element_type=jnp.float32,
        )
        / (ensemble - 1),
        "obs",
        scatter_dimension=0,
        tiled=True,
    )
    return members.astype(jnp.float32) + increment


def solution(mesh):
    in_specs = (P(("mem", "obs"), None), P(), P(), P("obs"), P("obs"), P("obs"), P("mem", "obs"))
    out_specs = P(("mem", "obs"), None)
    return jax.shard_map(shards, mesh=mesh, in_specs=in_specs, out_specs=out_specs, check_vma=False)
```

profile of v0, /device:TPU:1, one launch (start us, length us, event | category | flops | bytes accessed | tf_op | source)
XLA Modules:
  0.0 909.5 jit_solution(1563563488252477889)
XLA Ops:
  7.3 1.9 fusion.35
  16.7 2.1 fusion.5
  18.9 56.6 %all-gather.9.cloned.1.call-done = bf16[1024,4096]{1,0:T(8,128)(2,1)} async-done(((bf16[128,4096]{1,0:T(8,128)(2,1)}), bf16[1024,4096]{1,0:T(8,128)(2,1)}) %all-gather.9.cloned.1.call-update) | async-done | bytes 8388624 | tf_op jit(solution)/shard_map/all_gather | solution.py:79
  75.5 5.6 fusion.7
  81.2 7.9 all_to_all.19
  90.0 13.7 %all_gather.30 = bf16[64,4096]{1,0:T(8,128)(2,1)S(1)} all-gather(bf16[8,4096]{1,0:T(8,128)(2,1)S(1)} %copy-done.1), channel_id=1, replica_groups=mesh['mem'=32,'obs'=8] {'obs'}, dimensions={0}, use_global_device_ids=true | all-gather | bytes 589824 | tf_op jit(solution)/shard_map/all_gather | solution.py:70
  105.6 40.2 %all-gather = f32[131072]{0:T(1024)S(1)} all-gather(f32[4096]{0:T(1024)S(1)} %broadcast_multiply_fusion.2), channel_id=2, replica_groups=mesh['mem'=32,'obs'=8] {'mem'}, dimensions={0}, use_global_device_ids=true | all-gather | bytes 540672 | tf_op jit(solution)/shard_map/all_gather | solution.py:12
  147.4 58.7 %all-reduce = f32[32]{0:T(128)S(1)} all-reduce(f32[32]{0:T(128)S(1)} %dynamic-update-slice.3), channel_id=1, replica_groups=mesh['mem'=32,'obs'=8] {'mem'}, use_global_device_ids=true, to_apply=%add | all-reduce | flops 32 | bytes 256
  206.1 32.6 %all-gather.4 = f32[32,1,128]{2,1,0:T(1,128)S(1)} all-gather(f32[1,1,128]{2,1,0:T(1,128)S(1)} %get-tuple-element.340), channel_id=3, replica_groups=mesh['mem'=32,'obs'=8] {'mem'}, dimensions={0}, use_global_device_ids=true | all-gather | bytes 16896 | tf_op jit(solution)/shard_map/all_gather | solution.py:12
  239.6 359.1 %all-gather.11.cloned.1.call-done = f32[131072,128]{0,1:T(8,128)} async-done(((f32[4096,128]{0,1:T(8,128)}), f32[131072,128]{0,1:T(8,128)}) %all-gather.11.cloned.1.call-update) | async-done | bytes 67108880 | tf_op jit(solution)/shard_map/all_gather | solution.py:12
  598.7 3.1 slice.118
  603.7 65.7 %copy.14 = f32[131072,128]{1,0:T(8,128)} copy(f32[131072,128]{0,1:T(8,128)} %all-gather.11.cloned.1.call-done) | data formatting | bytes 134217728 | tf_op jit(solution)/shard_map/while | solution.py:18
  669.5 175.2 %while.23 = (s32[]{:T(128)}, f32[1]{0:T(128)}, f32[4096]{0:T(1024)S(1)}, f32[128]{0:T(128)S(1)}, f32[4096,128]{1,0:T(8,128)S(1)}, /*index=5*/f32[128,128]{1,0:T(...) while((s32[]{:T(128)}, f32[1]{0:T(128)}, ...), condition=%wide.region_3.0_spmd, body=%wide.region_2.0_spmd.sunk | while | flops 1638921 | bytes 6608147 | solution.py:18
  672.1 2.0 fusion.53
  677.8 2.0 fusion.53
  683.4 2.0 fusion.53
  689.1 2.0 fusion.53
  694.7 2.0 fusion.53
  700.4 2.0 fusion.53
  706.1 2.0 fusion.53
  711.7 2.0 fusion.53
  717.4 2.0 fusion.53
  723.0 2.0 fusion.53
  728.7 2.0 fusion.53
  734.3 2.0 fusion.53
  740.0 2.0 fusion.53
  745.6 2.0 fusion.53
  751.3 2.0 fusion.53
  756.9 2.0 fusion.53
  762.6 2.0 fusion.53
  768.2 2.0 fusion.53
  773.9 2.0 fusion.53
  779.5 2.0 fusion.53
  785.2 2.0 fusion.53
  790.8 2.0 fusion.53
  796.5 2.0 fusion.53
  802.1 2.0 fusion.53
  807.8 2.0 fusion.53
  813.4 2.0 fusion.53
  819.1 2.0 fusion.53
  824.7 2.0 fusion.53
  830.4 2.0 fusion.53
  836.0 2.0 fusion.53
  841.7 2.0 fusion.53
  845.0 11.7 %cholesky.16 = f32[128,128]{1,0:T(8,128)S(1)} custom-call(f32[128,128]{1,0:T(8,128)S(1)} %fusion.13), custom_call_target="Cholesky" | custom-call | tf_op jit(solution)/shard_map/jit(cholesky)/cholesky | solution.py:104
  858.1 9.8 %custom-call.10 = f32[1,128,128]{1,2,0:T(8,128)S(1)} custom-call(f32[1,128,128]{2,1,0:T(8,128)S(1)} %fusion.8), custom_call_target="InvertDiagBlocksLowerTriangular" | custom-call | tf_op jit(solution)/shard_map/jit(_cho_solve)/triangular_solve | solution.py:110
  868.4 3.3 convolution_multiply_fusion.7
  871.8 29.6 %reduce-scatter.2.cloned.1.call-done = f32[8,4096]{1,0:T(8,128)} async-done(((f32[64,4096]{1,0:T(8,128)}), f32[8,4096]{1,0:T(8,128)}) %reduce-scatter.2.cloned.1.call-update) | async-done | bytes 131088 | tf_op jit(solution)/shard_map/reduce_scatter | solution.py:111
  (245 shorter events, 67.8 us)
Async XLA Ops:
  6.5 69.0 %all-gather.9.cloned.1.call-start = ((), (), s32[]{:S(2)}) async-start(), calls=%async_computation.2 | async-start | bytes 9437184 | tf_op jit(solution)/shard_map/all_gather | solution.py:79
  16.7 58.9 %copy-start.1 = (bf16[8,4096]{1,0:T(8,128)(2,1)S(1)}, bf16[8,4096]{1,0:T(8,128)(2,1)}, u32[]{:S(2)}) copy-start(bf16[8,4096]{1,0:T(8,128)(2,1)} %param.9) | copy-start | bytes 196612
  18.8 219.9 %all-gather.13.cloned.1.call-start = ((), (), s32[]{:S(2)}) async-start(), calls=%async_computation.5 | async-start | bytes 2162688 | tf_op jit(solution)/shard_map/all_gather | solution.py:12
  90.0 508.7 %all-gather.11.cloned.1.call-start = ((), (), s32[]{:S(2)}) async-start(), calls=%async_computation.4 | async-start | bytes 69206016 | tf_op jit(solution)/shard_map/all_gather | solution.py:12
  105.6 40.4 %copy-start.6 = (u32[256]{0:T(256)S(1)}, u32[256]{0:T(256)}, u32[]{:S(2)}) copy-start(u32[256]{0:T(256)} %constant.128) | copy-start | bytes 3076
  105.6 100.5 %copy-start.4 = (f32[128]{0:T(128)S(1)}, f32[128]{0:T(128)}, u32[]{:S(2)}) copy-start(f32[128]{0:T(128)} %param.13) | copy-start | bytes 1540
  105.6 795.8 %reduce-scatter.2.cloned.1.call-start = ((), (), s32[]{:S(2)}) async-start(), calls=%async_computation.3 | async-start | bytes 1179648 | tf_op jit(solution)/shard_map/reduce_scatter | solution.py:111
  145.8 456.0 %copy-start = (f32[131072]{0:T(1024)}, f32[131072]{0:T(1024)S(1)}, u32[]{:S(2)}) copy-start(f32[131072]{0:T(1024)S(1)} %all-gather) | copy-start | bytes 1572868
  603.7 65.7 %slice-start = ((f32[131072]{0:T(1024)}), f32[4096]{0:T(1024)S(1)}, s32[]{:S(2)}) async-start(f32[131072]{0:T(1024)} %copy-done), calls=%async_computation.6 | async-start | bytes 32768 | tf_op jit(solution)/shard_map/slice | solution.py:13
  669.5 175.2 %copy-start.3 = (s32[128]{0:T(128)S(1)}, s32[128]{0:T(128)}, u32[]{:S(2)}) copy-start(s32[128]{0:T(128)} %param.12) | copy-start | bytes 1540
  669.5 198.4 %copy-start.2 = (bf16[64,128]{1,0:T(8,128)(2,1)S(1)}, bf16[64,128]{1,0:T(8,128)(2,1)}, u32[]{:S(2)}) copy-start(bf16[64,128]{1,0:T(8,128)(2,1)} %param.15) | copy-start | bytes 49156
  669.5 198.4 %copy-start.5 = (f32[128]{0:T(128)S(1)}, f32[128]{0:T(128)}, u32[]{:S(2)}) copy-start(f32[128]{0:T(128)} %param.14) | copy-start | bytes 1540
Sparse Core Ops, SparseCore 0:
  19.0 56.5 all-gather.8
  90.1 73.6 all-gather.12
  166.4 432.2 all-gather.10
  871.9 29.4 reduce-scatter.1
where the time goes:
time: 915 us; the launch traced here: 909 us
  waiting for transfers between devices  445 us (49%)
  blocking collectives  153 us (17%)
  other arithmetic  118 us (13%)
  local copies, waits for them, and re-layouts  94 us (10%)
  loops' own time  63.6 us (7%)
  matrix products  21.6 us (2%)
  between operations  13.4 us (1%)
    all_gather x2, waiting for transfers between devices, merged_2(): everything = jax.tree.map(lambda part: lax.all_gather(part, axis), array)  359 us
    all_gather x2, blocking collectives, merged_2(): everything = jax.tree.map(lambda part: lax.all_gather(part, axis), array)  72.8 us
    while x2, local copies, waits for them, and re-layouts, merged_2(): return lax.fori_loop(1, lax.axis_size(axis), lap, first)  67.6 us
    another operation x1, loops' own time, merged_2(): return lax.fori_loop(1, lax.axis_size(axis), lap, first)  63.6 us
    add x31, other arithmetic, combine_moments(): left_cross + right_cross  62.9 us
    unnamed x1, blocking collectives  58.7 us
    all_gather x1, waiting for transfers between devices, shards(): lax.all_gather(own_basis, 'obs', axis=0, tiled=True)  56.6 us
    reduce_scatter x1, waiting for transfers between devices, shards(): lax.psum_scatter(lax.dot_general(solved, cross_cov, (((0,), (1,)), ((), (...  29.6 us
  transfers between devices with their start and end apart: 4, of which 3 were waited for; matrix products, arithmetic and copies ran while one was open for 0% of the time, Pallas kernels for 0%

commit v1 on v0

v1 whole, which is shorter than its diff:
```python
import math

import jax
import jax.numpy as jnp
from jax import lax
from jax.experimental import pallas as pl
from jax.experimental.pallas import tpu as pltpu
from jax.sharding import PartitionSpec as P

ROWS = 8
TILE = 128
SLAB = 128
PANEL = 8
CHUNK = 256
F32 = jnp.float32
BF16 = jnp.bfloat16
FIRST = (((0,), (0,)), ((), ()))
LAST = (((1,), (1,)), ((), ()))
PLAIN = (((1,), (0,)), ((), ()))


def dot(left, right, dims, precision=None):
    return lax.dot_general(left, right, dims, precision=precision, preferred_element_type=F32)


def inverse(matrix):
    size = matrix.shape[0]
    row = lax.broadcasted_iota(jnp.int32, (PANEL, size), 0)
    lane = lax.broadcasted_iota(jnp.int32, (PANEL, size), 1)
    rest_lane = lax.broadcasted_iota(jnp.int32, (size - PANEL, size), 1)
    unit = jnp.where(lane == row, 1.0, 0.0).astype(F32)

    def block(_, full):
        top, rest = full[:PANEL], full[PANEL:]
        column = [jnp.broadcast_to(top[:, j : j + 1], (PANEL, size)) for j in range(PANEL)]
        panel = jnp.where(lane < PANEL, unit, top)
        for p in range(PANEL):
            scale = 1.0 / column[p][p : p + 1]
            pivot = panel[p : p + 1] * scale
            panel = jnp.where(row == p, pivot, panel - column[p] * pivot)
            for j in range(p + 1, PANEL):
                entry = column[j][p : p + 1] * scale
                column[j] = jnp.where(row == p, entry, column[j] - column[p] * entry)
        update = jnp.where(rest_lane < PANEL, 0.0, rest)
        for j in range(PANEL):
            update = update - rest[:, j : j + 1] * panel[j : j + 1]
        return pltpu.roll(jnp.concatenate([update, panel], axis=0), size - PANEL, 1)

    return lax.fori_loop(0, size // PANEL, block, matrix)


def kernel(
    nm,
    no,
    members,
    alphas,
    points,
    labels,
    noise,
    observed,
    perturb,
    out,
    rows,
    blocks_out,
    blocks_in,
    slabs,
    preds,
    perts,
    table,
    basis,
    innov,
    share_out,
    prior,
    incr_out,
    incr_in,
    final,
    coupled,
    spread,
    rows_s,
    rows_r,
    blocks_s,
    blocks_r,
    slabs_s,
    slabs_r,
    preds_s,
    preds_r,
    perts_s,
    perts_r,
    share_s,
    share_r,
    incr_s,
    incr_r,
):
    g, o = lax.axis_index("mem"), lax.axis_index("obs")
    y, c = lax.div(o, 2), lax.rem(o, 2)
    ny = no // 2
    coeffs = members.shape[1]
    half = coeffs // 2
    ensemble = nm * no * ROWS
    side = nm * ROWS

    def mem_peer(d):
        return lax.rem(g + d, nm)

    def obs_peer(d):
        return lax.rem(o + d, no)

    def y_peer(d):
        return lax.rem(y + d, ny) * 2 + c

    sibling = y * 2 + 1 - c

    def copy(src, dst, send, recv, to):
        return pltpu.make_async_remote_copy(
            src_ref=src, dst_ref=dst, send_sem=send, recv_sem=recv, device_id=to, device_id_type=pl.DeviceIdType.MESH
        )

    barrier = pltpu.get_barrier_semaphore()

    def greet_mem(d, carry):
        pl.semaphore_signal(barrier, inc=1, device_id=(mem_peer(d), o), device_id_type=pl.DeviceIdType.MESH)
        return carry

    def greet_obs(d, carry):
        pl.semaphore_signal(barrier, inc=1, device_id=(g, obs_peer(d)), device_id_type=pl.DeviceIdType.MESH)
        return carry

    lax.fori_loop(1, no, greet_obs, 0)
    lax.fori_loop(1, nm, greet_mem, 0)

    own = members[...].astype(F32)
    rows[o] = jnp.concatenate([own[:, :half], own[:, half:]], axis=0).astype(BF16)
    for k in range(nm):
        blocks_out[k] = own[:, k * SLAB : (k + 1) * SLAB]
    blocks_in[g] = blocks_out[g]
    perts[g] = perturb[...]

    at = points[:, pl.ds(pl.multiple_of(o * TILE, TILE), TILE)]
    turned = jnp.concatenate([at, jnp.zeros((TILE - at.shape[0], TILE), F32)], axis=0).T
    for d in range(at.shape[0]):
        x = jnp.broadcast_to(turned[:, d : d + 1], (TILE, TILE))
        second = x * x - 1.0
        third = x * second - 2.0 * x
        table[d, 0] = x
        table[d, 1] = second * (1.0 / math.sqrt(2.0))
        table[d, 2] = third * (1.0 / math.sqrt(6.0))

    label = jnp.broadcast_to(labels[...].astype(F32), (TILE, TILE))
    diagonal = lax.broadcasted_iota(jnp.int32, (TILE, TILE), 0) == lax.broadcasted_iota(jnp.int32, (TILE, TILE), 1)
    coupled[...] = jnp.where(label == label.T, 1.0 / (ensemble - 1), 0.0).astype(F32)
    spread[...] = jnp.where(diagonal, jnp.broadcast_to(noise[...], (TILE, TILE)), 0.0)

    pl.semaphore_wait(barrier, nm + no - 2)

    def send_rows(d):
        return copy(rows.at[o], rows.at[o], rows_s.at[d], rows_r.at[o], (g, y_peer(d)))

    def pass_rows(d):
        at = y_peer(d)
        return copy(rows.at[at], rows.at[at], rows_s.at[ny + d], rows_r.at[at], (g, sibling))

    own_rows = copy(rows.at[o], rows.at[o], rows_s.at[0], rows_r.at[o], (g, sibling))

    def take_rows(at):
        copy(rows.at[at], rows.at[at], rows_s.at[0], rows_r.at[at], (g, sibling)).wait_recv()

    for d in range(1, ny):
        send_rows(d).start()
    own_rows.start()

    def send_block(d):
        to = mem_peer(d)
        return copy(blocks_out.at[to], blocks_in.at[g], blocks_s.at[d], blocks_r.at[g], (to, o))

    def take_block(d):
        at = mem_peer(d)
        copy(blocks_out.at[at], blocks_in.at[at], blocks_s.at[d], blocks_r.at[at], (at, o)).wait_recv()

    def each(count, act):
        def step(d, carry):
            act(d)
            return carry

        lax.fori_loop(1, count, step, 0)

    each(nm, lambda d: send_block(d).start())

    def basis_chunk(part):
        def step(t, carry):
            first = pl.multiple_of(t * CHUNK, CHUNK)
            degree = alphas[:, pl.ds(pl.multiple_of(part * half + first, CHUNK), CHUNK)]
            product = None
            for d in range(degree.shape[0]):
                odd = (degree[d : d + 1] & 1) == 1
                high = degree[d : d + 1] >= 2
                one, two, three = (jnp.concatenate([table[d, q]] * (CHUNK // TILE), axis=1) for q in range(3))
                value = jnp.where(high, jnp.where(odd, three, two), jnp.where(odd, one, 1.0))
                product = value if product is None else product * value
            basis[pl.ds(part * TILE, TILE), pl.ds(first, CHUNK)] = product.astype(BF16)
            return carry

        lax.fori_loop(0, half // CHUNK, step, 0)

    basis_chunk(0)
    for d in range(1, ny):
        take_rows(y_peer(d))
        pass_rows(d).start()
    basis_chunk(1)
    take_rows(sibling)
    for d in range(1, ny):
        take_rows(lax.rem(y + d, ny) * 2 + 1 - c)

    both = dot(rows[...].reshape(no * 2 * ROWS, half), basis[...], LAST)
    both = both.reshape(no, 2, ROWS, 2 * TILE)
    mine = (both[:, 0, :, :TILE] + both[:, 1, :, TILE:]).reshape(no * ROWS, TILE)
    preds[g] = mine.astype(BF16)

    def send_pred(d):
        return copy(preds.at[g], preds.at[g], preds_s.at[d], preds_r.at[g], (mem_peer(d), o))

    def take_pred(d):
        at = mem_peer(d)
        copy(preds.at[at], preds.at[at], preds_s.at[d], preds_r.at[at], (at, o)).wait_recv()

    def send_pert(d):
        return copy(perts.at[g], perts.at[g], perts_s.at[d], perts_r.at[g], (mem_peer(d), o))

    def take_pert(d):
        at = mem_peer(d)
        copy(perts.at[at], perts.at[at], perts_s.at[d], perts_r.at[at], (at, o)).wait_recv()

    each(nm, lambda d: send_pred(d).start())

    each(nm, take_block)
    slabs[o] = blocks_in[...].reshape(side, SLAB).astype(BF16)

    def send_slab(d):
        return copy(slabs.at[o], slabs.at[o], slabs_s.at[d], slabs_r.at[o], (g, y_peer(d)))

    def pass_slab(d):
        at = y_peer(d)
        return copy(slabs.at[at], slabs.at[at], slabs_s.at[ny + d], slabs_r.at[at], (g, sibling))

    own_slab = copy(slabs.at[o], slabs.at[o], slabs_s.at[0], slabs_r.at[o], (g, sibling))

    def take_slab(at):
        copy(slabs.at[at], slabs.at[at], slabs_s.at[0], slabs_r.at[at], (g, sibling)).wait_recv()

    for d in range(1, ny):
        send_slab(d).start()
    own_slab.start()
    each(nm, lambda d: send_pert(d).start())

    each(nm, take_pred)
    flat = preds[...].reshape(ensemble, TILE)
    ones = jnp.ones((2 * ROWS, ensemble), BF16)
    mean_pred = jnp.broadcast_to(dot(ones, flat, PLAIN)[:1] / ensemble, (TILE, TILE))
    mean_turned = mean_pred.T
    gram = dot(flat, flat, FIRST) - ensemble * mean_turned * mean_pred
    system = gram * coupled[...] + spread[...]

    for d in range(1, ny):
        take_slab(y_peer(d))
        pass_slab(d).start()

    inverted = inverse(system)

    each(nm, take_pert)
    noise_root = jnp.sqrt(noise[...])

    def innovate(t, carry):
        value = preds[t].astype(F32)
        left = observed[...] + noise_root * perts[t].astype(F32) - value
        for k in range(no):
            innov[k, pl.ds(pl.multiple_of(t * ROWS, ROWS), ROWS), :] = left[k * ROWS : (k + 1) * ROWS]
            prior[k, pl.ds(pl.multiple_of(t * ROWS, ROWS), ROWS), :] = value[k * ROWS : (k + 1) * ROWS]
        return carry

    lax.fori_loop(0, nm, innovate, 0)
    ordered = prior[...].reshape(ensemble, TILE).astype(BF16)

    take_slab(sibling)
    for d in range(1, ny):
        take_slab(lax.rem(y + d, ny) * 2 + 1 - c)
    slab = slabs[...].reshape(ensemble, SLAB)
    mean_param = jnp.broadcast_to(dot(ones, slab, PLAIN)[:1] / ensemble, (TILE, SLAB))
    cross = dot(ordered, slab, FIRST) - ensemble * mean_turned * mean_param
    gain = dot(inverted, cross, PLAIN, lax.Precision.HIGHEST) / (ensemble - 1)
    high = gain.astype(BF16)
    low = (gain - high.astype(F32)).astype(BF16)
    weights = jnp.concatenate([high, low], axis=1)
    weights = jnp.concatenate([weights, weights], axis=0)

    def send_share(d):
        to = obs_peer(d)
        return copy(share_out.at[to], incr_in.at[o], share_s.at[d], share_r.at[o], (g, to))

    def take_share(d):
        at = obs_peer(d)
        copy(share_out.at[at], incr_in.at[at], share_s.at[d], share_r.at[at], (g, at)).wait_recv()

    def share(at):
        left = innov[at]
        big = left.astype(BF16)
        small = (left - big.astype(F32)).astype(BF16)
        parts = dot(jnp.concatenate([big, small], axis=1), weights, PLAIN)
        return parts[:, :SLAB] + parts[:, SLAB:]

    for d in range(1, no):
        to = obs_peer(d)
        share_out[to] = share(to).astype(BF16)
        send_share(d).start()
    total = share(o)
    for d in range(1, no):
        take_share(d)
        total = total + incr_in[obs_peer(d)].astype(F32)
    incr_out[...] = total.reshape(nm, ROWS, SLAB)

    def send_incr(d):
        to = mem_peer(d)
        return copy(incr_out.at[to], final.at[g], incr_s.at[d], incr_r.at[g], (to, o))

    def take_incr(d):
        at = mem_peer(d)
        copy(incr_out.at[at], final.at[at], incr_s.at[d], incr_r.at[at], (at, o)).wait_recv()

    each(nm, lambda d: send_incr(d).start())
    final[g] = incr_out[g]
    each(nm, take_incr)
    for k in range(nm):
        out[:, k * SLAB : (k + 1) * SLAB] = own[:, k * SLAB : (k + 1) * SLAB] + final[k]

    for d in range(1, ny):
        send_rows(d).wait_send()
        pass_rows(d).wait_send()
        send_slab(d).wait_send()
        pass_slab(d).wait_send()
    own_rows.wait_send()
    own_slab.wait_send()
    for d in range(1, no):
        send_share(d).wait_send()

    def sent(d):
        send_block(d).wait_send()
        send_pred(d).wait_send()
        send_pert(d).wait_send()
        send_incr(d).wait_send()

    each(nm, sent)


def shards(members, alphas, points, labels, noise, observed, perturb):
    nm, no = lax.axis_size("mem"), lax.axis_size("obs")
    coeffs = members.shape[1]
    side = nm * ROWS
    vmem = pl.BlockSpec(memory_space=pltpu.VMEM)
    many = pltpu.SemaphoreType.DMA
    return pl.pallas_call(
        lambda *refs: kernel(nm, no, *refs),
        out_shape=jax.ShapeDtypeStruct((ROWS, coeffs), F32),
        in_specs=[vmem] * 7,
        out_specs=vmem,
        scratch_shapes=[
            pltpu.VMEM((no, 2 * ROWS, coeffs // 2), BF16),
            pltpu.VMEM((nm, ROWS, SLAB), F32),
            pltpu.VMEM((nm, ROWS, SLAB), F32),
            pltpu.VMEM((no, side, SLAB), BF16),
            pltpu.VMEM((nm, no * ROWS, TILE), BF16),
            pltpu.VMEM((nm, no * ROWS, TILE), BF16),
            pltpu.VMEM((alphas.shape[0], 3, TILE, TILE), F32),
            pltpu.VMEM((2 * TILE, coeffs // 2), BF16),
            pltpu.VMEM((no, side, TILE), F32),
            pltpu.VMEM((no, side, SLAB), BF16),
            pltpu.VMEM((no, side, TILE), F32),
            pltpu.VMEM((nm, ROWS, SLAB), F32),
            pltpu.VMEM((no, side, SLAB), BF16),
            pltpu.VMEM((nm, ROWS, SLAB), F32),
            pltpu.VMEM((TILE, TILE), F32),
            pltpu.VMEM((TILE, TILE), F32),
            many((no,)),
            many((no,)),
            many((nm,)),
            many((nm,)),
            many((no,)),
            many((no,)),
            many((nm,)),
            many((nm,)),
            many((nm,)),
            many((nm,)),
            many((no,)),
            many((no,)),
            many((nm,)),
            many((nm,)),
        ],
        compiler_params=pltpu.CompilerParams(
            collective_id=0, has_side_effects=True, vmem_limit_bytes=40 * 1024 * 1024
        ),
    )(members, alphas, points, labels.reshape(1, TILE), noise.reshape(1, TILE), observed.reshape(1, TILE), perturb)


def solution(mesh):
    in_specs = (P(("mem", "obs"), None), P(), P(), P("obs"), P("obs"), P("obs"), P("mem", "obs"))
    out_specs = P(("mem", "obs"), None)
    return jax.shard_map(shards, mesh=mesh, in_specs=in_specs, out_specs=out_specs, check_vma=False)
```

time: 915 us -> 67.4 us (0.07)
  waiting for transfers between devices: 445 us -> 0 us
  blocking collectives: 153 us -> 0 us
  other arithmetic: 118 us -> 0 us
  local copies, waits for them, and re-layouts: 94 us -> 4.56 us
  loops' own time: 63.6 us -> 0 us
  Pallas kernels: 0 us -> 62.5 us
  matrix products: 21.6 us -> 0 us
  between operations: 13.4 us -> 0.02 us
    all_gather x3 -> x0, waiting for transfers between devices: 416 us -> none  [the longest x2 359 us: merged_2(): everything = jax.tree.map(lambda part: lax.all_gather(part, axis), array)]
    add x95 -> x0, other arithmetic: 93.7 us -> none  [the longest x31 62.9 us: combine_moments(): left_cross + right_cross]
    all_gather x3 -> x0, blocking collectives: 86.4 us -> none  [the longest x2 72.8 us: merged_2(): everything = jax.tree.map(lambda part: lax.all_gather(part, axis), array)]
    while x2 -> x0, local copies, waits for them, and re-layouts: 67.6 us -> none  [merged_2(): return lax.fori_loop(1, lax.axis_size(axis), lap, first)]
    another operation x1 -> x0, loops' own time: 63.6 us -> none  [merged_2(): return lax.fori_loop(1, lax.axis_size(axis), lap, first)]
    pallas_call x0 -> x1, Pallas kernels: none -> 62.5 us  [shards(): pl.pallas_call(lambda *refs: kernel(nm, no, *refs), out_shape=jax.ShapeDt...]
    unnamed x1 -> x0, blocking collectives: 58.7 us -> none
    reduce_scatter x1 -> x0, waiting for transfers between devices: 29.6 us -> none  [shards(): lax.psum_scatter(lax.dot_general(solved, cross_cov, (((0,), (1,)), ((), (...]
  transfers between devices with their start and end apart: 4 -> 0, of which waited for: 3 -> 0; matrix products, arithmetic and copies ran while one was open for 0% -> 0% of each run, Pallas kernels for 0% -> 0%
where the time goes in v1:
time: 67.4 us; the launch traced here: 67.1 us
  Pallas kernels  62.5 us (93%)
  local copies, waits for them, and re-layouts  4.56 us (7%)
    pallas_call x1, Pallas kernels, shards(): pl.pallas_call(lambda *refs: kernel(nm, no, *refs), out_shape=jax.ShapeDt...  62.5 us
    unnamed x15, local copies, waits for them, and re-layouts  4.56 us

profile of v1, /device:TPU:1, one launch (start us, length us, event | category | flops | bytes accessed | tf_op | source)
XLA Modules:
  0.0 67.1 jit_solution(5461907055341489682)
XLA Ops:
  0.0 0.0 copy-start.4
  0.0 0.0 copy-start.5
  0.0 0.0 copy-start.6
  0.0 0.6 copy-done.4
  0.7 0.0 copy-done.5
  0.7 0.0 copy-done.6
  0.7 0.0 copy-start
  0.7 0.9 %copy-done = s32[8,4096]{1,0:T(8,128)S(1)} copy-done((s32[8,4096]{1,0:T(8,128)S(1)}, s32[8,4096]{1,0:T(8,128)}, u32[]{:S(2)}) %copy-start) | copy-done | bytes 131096
  1.6 0.0 copy-start.1
  1.6 0.8 %copy-done.1 = bf16[8,4096]{1,0:T(8,128)(2,1)S(1)} copy-done((bf16[8,4096]{1,0:T(8,128)(2,1)S(1)}, bf16[8,4096]{1,0:T(8,128)(2,1)}, u32[]{:S(2)}) %copy-start.1) | copy-done | bytes 65560
  2.4 0.0 copy-start.2
  2.4 0.8 %copy-done.2 = f32[8,1024]{1,0:T(8,128)S(1)} copy-done((f32[8,1024]{1,0:T(8,128)S(1)}, f32[8,1024]{1,0:T(8,128)}, u32[]{:S(2)}) %copy-start.2) | copy-done | bytes 32792
  3.2 0.0 copy-start.3
  3.2 0.7 %copy-done.3 = bf16[64,128]{1,0:T(8,128)(2,1)S(1)} copy-done((bf16[64,128]{1,0:T(8,128)(2,1)S(1)}, bf16[64,128]{1,0:T(8,128)(2,1)}, u32[]{:S(2)}) %copy-start.3) | copy-done | bytes 16408
  3.9 62.5 %shard_map.73 = f32[8,4096]{1,0:T(8,128)S(1)} custom-call(bf16[8,4096]{1,0:T(8,128)(2,1)S(1)} %copy-done.1, s32[8,4096]{1,0:T(8,128)S(1)} %copy-done, f32[8,1024]{1,0:T(8,128)S(1)} %copy-done.2, s32[1,128]{1,0:T(1,128)S(1)} %bitcast.3, f32[1,128]{1,0:T(1,128)S(1)} %bitcast.4, f32[1,128]{1,0:T(1,128)S(1)} %bitcast.5, bf16[64,128]{1,0:T(8,128)(2,1)S(1)} %copy-done.3), custom_call_target="tpu_custom_call" | custom-call | tf_op jit(solution)/shard_map/pallas_call | solution.py:358
  66.4 0.7 copy.9
Async XLA Ops:
  0.0 0.7 copy-start.4
  0.0 0.7 copy-start.5
  0.0 0.7 %copy-start.6 = (f32[128]{0:T(128)S(1)}, f32[128]{0:T(128)}, u32[]{:S(2)}) copy-start(f32[128]{0:T(128)} %param.12) | copy-start | bytes 1540
  0.7 0.9 %copy-start = (s32[8,4096]{1,0:T(8,128)S(1)}, s32[8,4096]{1,0:T(8,128)}, u32[]{:S(2)}) copy-start(s32[8,4096]{1,0:T(8,128)} %refs_1_.1) | copy-start | bytes 393220
  1.6 0.8 %copy-start.1 = (bf16[8,4096]{1,0:T(8,128)(2,1)S(1)}, bf16[8,4096]{1,0:T(8,128)(2,1)}, u32[]{:S(2)}) copy-start(bf16[8,4096]{1,0:T(8,128)(2,1)} %refs_0_.1) | copy-start | bytes 196612
  2.4 0.8 %copy-start.2 = (f32[8,1024]{1,0:T(8,128)S(1)}, f32[8,1024]{1,0:T(8,128)}, u32[]{:S(2)}) copy-start(f32[8,1024]{1,0:T(8,128)} %refs_2_.1) | copy-start | bytes 98308
  3.2 0.7 %copy-start.3 = (bf16[64,128]{1,0:T(8,128)(2,1)S(1)}, bf16[64,128]{1,0:T(8,128)(2,1)}, u32[]{:S(2)}) copy-start(bf16[64,128]{1,0:T(8,128)(2,1)} %refs_6_.1) | copy-start | bytes 49156

commit v2 on v1

v2 whole, which is shorter than its diff:
```python
import math

import jax
import jax.numpy as jnp
from jax import lax
from jax.experimental import pallas as pl
from jax.experimental.pallas import tpu as pltpu
from jax.sharding import PartitionSpec as P

ROWS = 8
TILE = 128
SLAB = 128
PANEL = 8
CHUNK = 256
NX = 4
F32 = jnp.float32
BF16 = jnp.bfloat16
FIRST = (((0,), (0,)), ((), ()))
LAST = (((1,), (1,)), ((), ()))
PLAIN = (((1,), (0,)), ((), ()))


def dot(left, right, dims, precision=None):
    return lax.dot_general(left, right, dims, precision=precision, preferred_element_type=F32)


def inverse(matrix):
    size = matrix.shape[0]
    row = lax.broadcasted_iota(jnp.int32, (PANEL, size), 0)
    lane = lax.broadcasted_iota(jnp.int32, (PANEL, size), 1)
    rest_lane = lax.broadcasted_iota(jnp.int32, (size - PANEL, size), 1)
    unit = jnp.where(lane == row, 1.0, 0.0).astype(F32)

    def block(_, full):
        top, rest = full[:PANEL], full[PANEL:]
        column = [jnp.broadcast_to(top[:, j : j + 1], (PANEL, size)) for j in range(PANEL)]
        panel = jnp.where(lane < PANEL, unit, top)
        for p in range(PANEL):
            scale = 1.0 / column[p][p : p + 1]
            pivot = panel[p : p + 1] * scale
            panel = jnp.where(row == p, pivot, panel - column[p] * pivot)
            for j in range(p + 1, PANEL):
                entry = column[j][p : p + 1] * scale
                column[j] = jnp.where(row == p, entry, column[j] - column[p] * entry)
        update = jnp.where(rest_lane < PANEL, 0.0, rest)
        for j in range(PANEL):
            update = update - rest[:, j : j + 1] * panel[j : j + 1]
        return pltpu.roll(jnp.concatenate([update, panel], axis=0), size - PANEL, 1)

    return lax.fori_loop(0, size // PANEL, block, matrix)


def kernel(
    nm,
    no,
    members_hbm,
    alphas_hbm,
    points_hbm,
    labels_hbm,
    noise_hbm,
    observed_hbm,
    perturb_hbm,
    out,
    members,
    alphas,
    points,
    labels,
    noise,
    observed,
    rows_out,
    rows_in,
    halves,
    half_in,
    blocks_out,
    blocks_in,
    slabs,
    preds,
    perts,
    grams,
    table,
    basis,
    innov,
    prior,
    pair_out,
    pair_in,
    share_out,
    share_in,
    incr_out,
    final,
    coupled,
    spread,
    local_s,
    rows_s,
    rows_r,
    half_s,
    half_r,
    blocks_s,
    blocks_r,
    slabs_s,
    slabs_r,
    preds_s,
    preds_r,
    lines_s,
    lines_r,
    perts_s,
    perts_r,
    extra_s,
    extra_r,
    grams_s,
    grams_r,
    pair_s,
    pair_r,
    share_s,
    share_r,
    incr_s,
    incr_r,
):
    g, o = lax.axis_index("mem"), lax.axis_index("obs")
    z, x = lax.div(g, NX), lax.rem(g, NX)
    y, c = lax.div(o, 2), lax.rem(o, 2)
    nz, ny = nm // NX, no // 2
    coeffs = members.shape[1]
    half = coeffs // 2
    quarter = half // 2
    chunk = min(CHUNK, quarter)
    ensemble = nm * no * ROWS
    line = nz * no * ROWS
    side = nm * ROWS
    slot = x * nz + z
    mesh = pl.DeviceIdType.MESH

    def mem_at(d):
        return lax.rem(g + d, nm)

    def slot_at(at):
        return lax.rem(at, NX) * nz + lax.div(at, NX)

    def obs_at(d):
        return lax.rem(o + d, no)

    def z_at(d):
        return lax.rem(z + d, nz)

    def x_at(d):
        return lax.rem(x + d, NX)

    def y_at(d):
        return lax.rem(y + d, ny)

    sibling = y * 2 + 1 - c

    def copy(src, dst, send, recv, to):
        return pltpu.make_async_remote_copy(
            src_ref=src, dst_ref=dst, send_sem=send, recv_sem=recv, device_id=to, device_id_type=mesh
        )

    def each(count, act):
        def step(d, carry):
            act(d)
            return carry

        lax.fori_loop(1, count, step, 0)

    fetch = [
        pltpu.make_async_copy(src, dst, local_s.at[k])
        for k, (src, dst) in enumerate(
            (
                (members_hbm, members),
                (points_hbm.at[:, pl.ds(pl.multiple_of(y * 2 * TILE, 2 * TILE), 2 * TILE)], points),
                (labels_hbm, labels),
                (noise_hbm, noise),
                (observed_hbm, observed),
                (perturb_hbm, perts.at[slot]),
                (alphas_hbm, alphas),
            )
        )
    ]
    for f in fetch:
        f.start()

    barrier = pltpu.get_barrier_semaphore()
    each(no, lambda d: pl.semaphore_signal(barrier, inc=1, device_id=(g, obs_at(d)), device_id_type=mesh))
    each(nm, lambda d: pl.semaphore_signal(barrier, inc=1, device_id=(mem_at(d), o), device_id_type=mesh))

    fetch[0].wait()
    own = members[...].astype(F32)
    for h in range(2):
        part = own[:, h * half : (h + 1) * half]
        rows_out[h] = jnp.concatenate([part[:, :quarter], part[:, quarter:]], axis=0).astype(BF16)
    rows_in[o] = rows_out[c]
    for k in range(nm):
        blocks_out[k] = own[:, k * SLAB : (k + 1) * SLAB]
    blocks_in[slot] = blocks_out[g]

    fetch[1].wait()
    for t in range(2):
        at = points[:, t * TILE : (t + 1) * TILE]
        turned = jnp.concatenate([at, jnp.zeros((TILE - at.shape[0], TILE), F32)], axis=0).T
        for d in range(at.shape[0]):
            value = jnp.broadcast_to(turned[:, d : d + 1], (TILE, TILE))
            second = value * value - 1.0
            third = value * second - 2.0 * value
            table[t, d, 0] = value
            table[t, d, 1] = second * (1.0 / math.sqrt(2.0))
            table[t, d, 2] = third * (1.0 / math.sqrt(6.0))

    for f in fetch[2:]:
        f.wait()
    label = jnp.broadcast_to(labels[...].astype(F32), (TILE, TILE))
    diagonal = lax.broadcasted_iota(jnp.int32, (TILE, TILE), 0) == lax.broadcasted_iota(jnp.int32, (TILE, TILE), 1)
    coupled[...] = jnp.where(label == label.T, 1.0 / (ensemble - 1), 0.0).astype(F32)
    spread[...] = jnp.where(diagonal, jnp.broadcast_to(noise[...], (TILE, TILE)), 0.0)

    pl.semaphore_wait(barrier, nm + no - 2)

    def rows_to(d):
        to = obs_at(d)
        return copy(rows_out.at[lax.rem(to, 2)], rows_in.at[o], rows_s.at[d], rows_r.at[o], (g, to))

    def rows_from(d):
        at = obs_at(d)
        return copy(rows_out.at[c], rows_in.at[at], rows_s.at[d], rows_r.at[at], (g, at))

    each(no, lambda d: rows_to(d).start())

    def pert_to(d):
        return copy(perts.at[slot], perts.at[slot], perts_s.at[d], perts_r.at[z], (z_at(d) * NX + x, o))

    def pert_from(d):
        at = x * nz + z_at(d)
        return copy(perts.at[at], perts.at[at], perts_s.at[d], perts_r.at[z_at(d)], (z_at(d) * NX + x, o))

    each(nz, lambda d: pert_to(d).start())

    def block_to(d):
        to = mem_at(d)
        return copy(blocks_out.at[to], blocks_in.at[slot], blocks_s.at[d], blocks_r.at[slot], (to, o))

    def block_from(d):
        at = mem_at(d)
        place = slot_at(at)
        return copy(blocks_out.at[at], blocks_in.at[place], blocks_s.at[d], blocks_r.at[place], (at, o))

    each(nm, lambda d: block_to(d).start())

    def basis_part(q):
        def step(n, carry):
            t, k = lax.div(n, quarter // chunk), lax.rem(n, quarter // chunk)
            first = pl.multiple_of(k * chunk, chunk)
            degree = alphas[:, pl.ds(pl.multiple_of(c * half + q * quarter + first, chunk), chunk)]
            product = None
            for d in range(degree.shape[0]):
                odd = (degree[d : d + 1] & 1) == 1
                high = degree[d : d + 1] >= 2
                one, two, three = (jnp.concatenate([table[t, d, p]] * (chunk // TILE), axis=1) for p in range(3))
                value = jnp.where(high, jnp.where(odd, three, two), jnp.where(odd, one, 1.0))
                product = value if product is None else product * value
            place = pl.multiple_of((q * 2 + t) * TILE, TILE)
            basis[pl.ds(place, TILE), pl.ds(first, chunk)] = product.astype(BF16)
            return carry

        lax.fori_loop(0, 2 * (quarter // chunk), step, 0)

    def line_to(buffer, send, recv, d):
        span = buffer.at[pl.ds(x * nz, nz)]
        return copy(span, span, send.at[d], recv.at[x], (z * NX + x_at(d), o))

    def line_from(buffer, send, recv, d):
        span = buffer.at[pl.ds(x_at(d) * nz, nz)]
        return copy(span, span, send.at[d], recv.at[x_at(d)], (z * NX + x_at(d), o))

    basis_part(0)
    each(nz, lambda d: pert_from(d).wait_recv())
    each(NX, lambda d: line_to(perts, extra_s, extra_r, d).start())
    basis_part(1)

    each(no, lambda d: rows_from(d).wait_recv())
    both = dot(rows_in[...].reshape(no * 2 * ROWS, quarter), basis[...], LAST)
    both = both.reshape(no, 2, ROWS, 4 * TILE)
    part = (both[:, 0, :, : 2 * TILE] + both[:, 1, :, 2 * TILE :]).reshape(no * ROWS, 2 * TILE)
    for t in range(2):
        halves[t] = part[:, t * TILE : (t + 1) * TILE]
    half_copy = copy(halves.at[1 - c], half_in, half_s, half_r, (g, sibling))
    half_copy.start()
    half_copy.wait_recv()
    preds[slot] = (halves[c] + half_in[...]).astype(BF16)

    def pred_to(d):
        return copy(preds.at[slot], preds.at[slot], preds_s.at[d], preds_r.at[z], (z_at(d) * NX + x, o))

    def pred_from(d):
        at = x * nz + z_at(d)
        return copy(preds.at[at], preds.at[at], preds_s.at[d], preds_r.at[z_at(d)], (z_at(d) * NX + x, o))

    each(nz, lambda d: pred_to(d).start())

    each(nm, lambda d: block_from(d).wait_recv())
    slabs[o] = blocks_in[...].reshape(side, SLAB).astype(BF16)

    def slab_to(d):
        return copy(slabs.at[o], slabs.at[o], slabs_s.at[d], slabs_r.at[o], (g, y_at(d) * 2 + c))

    def slab_from(at, to):
        return copy(slabs.at[at], slabs.at[at], slabs_s.at[0], slabs_r.at[at], (g, to))

    def slab_pass(d):
        at = y_at(d) * 2 + c
        return copy(slabs.at[at], slabs.at[at], slabs_s.at[ny + d], slabs_r.at[at], (g, sibling))

    slab_own = copy(slabs.at[o], slabs.at[o], slabs_s.at[0], slabs_r.at[o], (g, sibling))
    each(ny, lambda d: slab_to(d).start())
    slab_own.start()

    each(nz, lambda d: pred_from(d).wait_recv())
    flat = preds[pl.ds(x * nz, nz)].reshape(line, TILE)
    ones = jnp.ones((2 * ROWS, ensemble), BF16)
    grams[x, :TILE] = dot(flat, flat, FIRST)
    grams[x, TILE:] = dot(ones[:, :line], flat, PLAIN)[:ROWS]

    def gram_to(d):
        return copy(grams.at[x], grams.at[x], grams_s.at[d], grams_r.at[x], (z * NX + x_at(d), o))

    def gram_from(d):
        at = x_at(d)
        return copy(grams.at[at], grams.at[at], grams_s.at[d], grams_r.at[at], (z * NX + at, o))

    each(NX, lambda d: gram_to(d).start())
    each(NX, lambda d: line_to(preds, lines_s, lines_r, d).start())

    def pass_on(d):
        at = y_at(d) * 2 + c
        slab_from(at, at).wait_recv()
        slab_pass(d).start()

    each(ny, pass_on)

    each(NX, lambda d: gram_from(d).wait_recv())
    gram = grams[0]
    for k in range(1, NX):
        gram = gram + grams[k]
    mean_pred = jnp.broadcast_to(gram[TILE : TILE + 1] / ensemble, (TILE, TILE))
    mean_turned = mean_pred.T
    system = (gram[:TILE] - ensemble * mean_turned * mean_pred) * coupled[...] + spread[...]

    inverted = inverse(system)

    each(NX, lambda d: line_from(perts, extra_s, extra_r, d).wait_recv())
    each(NX, lambda d: line_from(preds, lines_s, lines_r, d).wait_recv())
    noise_root = jnp.sqrt(noise[...])

    def innovate(t, carry):
        value = preds[t].astype(F32)
        left = observed[...] + noise_root * perts[t].astype(F32) - value
        place = pl.ds(pl.multiple_of(t * ROWS, ROWS), ROWS)
        for k in range(no):
            innov[k, place, :] = left[k * ROWS : (k + 1) * ROWS]
            prior[k, place, :] = value[k * ROWS : (k + 1) * ROWS]
        return carry

    lax.fori_loop(0, nm, innovate, 0)
    ordered = prior[...].reshape(ensemble, TILE).astype(BF16)

    slab_from(sibling, sibling).wait_recv()
    each(ny, lambda d: slab_from(y_at(d) * 2 + 1 - c, sibling).wait_recv())
    slab = slabs[...].reshape(ensemble, SLAB)
    mean_param = jnp.broadcast_to(dot(ones, slab, PLAIN)[:1] / ensemble, (TILE, SLAB))
    cross = dot(ordered, slab, FIRST) - ensemble * mean_turned * mean_param
    gain = dot(inverted, cross, PLAIN, lax.Precision.HIGHEST) / (ensemble - 1)
    high = gain.astype(BF16)
    low = (gain - high.astype(F32)).astype(BF16)
    weights = jnp.concatenate([high, low], axis=1)
    weights = jnp.concatenate([weights, weights], axis=0)

    def share(at):
        left = innov[at]
        big = left.astype(BF16)
        small = (left - big.astype(F32)).astype(BF16)
        parts = dot(jnp.concatenate([big, small], axis=1), weights, PLAIN)
        return parts[:, :SLAB] + parts[:, SLAB:]

    def pair_copy(d):
        at = y_at(d)
        return copy(pair_out.at[d], pair_in.at[d], pair_s.at[d], pair_r.at[d], (g, sibling))

    def share_to(d):
        return copy(share_out.at[d], share_in.at[y], share_s.at[d], share_r.at[y], (g, y_at(d) * 2 + c))

    def share_from(d):
        at = y_at(d)
        return copy(share_out.at[d], share_in.at[at], share_s.at[d], share_r.at[at], (g, at * 2 + c))

    turns = sorted(range(1, ny), key=lambda d: -min(d, ny - d)) + [0]
    for d in turns:
        pair_out[d] = share(y_at(d) * 2 + 1 - c).astype(BF16)
        pair_copy(d).start()
    for d in turns:
        total = share(y_at(d) * 2 + c)
        pair_copy(d).wait_recv()
        total = total + pair_in[d].astype(F32)
        if d:
            share_out[d] = total.astype(BF16)
            share_to(d).start()
    for d in turns[:-1]:
        share_from(d).wait_recv()
        total = total + share_in[y_at(d)].astype(F32)
    incr_out[...] = total.reshape(nm, ROWS, SLAB)

    def incr_to(d):
        to = mem_at(d)
        return copy(incr_out.at[slot_at(to)], final.at[g], incr_s.at[d], incr_r.at[g], (to, o))

    def incr_from(d):
        at = mem_at(d)
        return copy(incr_out.at[slot_at(at)], final.at[at], incr_s.at[d], incr_r.at[at], (at, o))

    each(nm, lambda d: incr_to(d).start())
    final[g] = incr_out[slot]
    each(nm, lambda d: incr_from(d).wait_recv())
    for k in range(nm):
        at = slice(k * SLAB, (k + 1) * SLAB)
        out[:, at] = members[:, at].astype(F32) + final[k]

    def obs_sent(d):
        rows_to(d).wait_send()

    def y_sent(d):
        slab_to(d).wait_send()
        slab_pass(d).wait_send()
        share_to(d).wait_send()
        pair_copy(d).wait_send()

    def z_sent(d):
        pert_to(d).wait_send()
        pred_to(d).wait_send()

    def x_sent(d):
        gram_to(d).wait_send()
        line_to(perts, extra_s, extra_r, d).wait_send()
        line_to(preds, lines_s, lines_r, d).wait_send()

    def mem_sent(d):
        block_to(d).wait_send()
        incr_to(d).wait_send()

    half_copy.wait_send()
    slab_own.wait_send()
    pair_copy(0).wait_send()
    each(no, obs_sent)
    each(ny, y_sent)
    each(nz, z_sent)
    each(NX, x_sent)
    each(nm, mem_sent)


def shards(members, alphas, points, labels, noise, observed, perturb):
    nm, no = lax.axis_size("mem"), lax.axis_size("obs")
    nz, ny = nm // NX, no // 2
    coeffs = members.shape[1]
    dims = alphas.shape[0]
    side = nm * ROWS
    vmem, many = pltpu.VMEM, pltpu.SemaphoreType.DMA
    return pl.pallas_call(
        lambda *refs: kernel(nm, no, *refs),
        out_shape=jax.ShapeDtypeStruct((ROWS, coeffs), F32),
        in_specs=[pl.BlockSpec(memory_space=pl.ANY)] * 7,
        out_specs=pl.BlockSpec(memory_space=vmem),
        scratch_shapes=[
            vmem((ROWS, coeffs), BF16),
            vmem((dims, coeffs), jnp.int32),
            vmem((dims, 2 * TILE), F32),
            vmem((1, TILE), jnp.int32),
            vmem((1, TILE), F32),
            vmem((1, TILE), F32),
            vmem((2, 2 * ROWS, coeffs // 4), BF16),
            vmem((no, 2 * ROWS, coeffs // 4), BF16),
            vmem((2, no * ROWS, TILE), F32),
            vmem((no * ROWS, TILE), F32),
            vmem((nm, ROWS, SLAB), F32),
            vmem((nm, ROWS, SLAB), F32),
            vmem((no, side, SLAB), BF16),
            vmem((nm, no * ROWS, TILE), BF16),
            vmem((nm, no * ROWS, TILE), BF16),
            vmem((NX, TILE + ROWS, TILE), F32),
            vmem((2, dims, 3, TILE, TILE), F32),
            vmem((4 * TILE, coeffs // 4), BF16),
            vmem((no, side, TILE), F32),
            vmem((no, side, TILE), F32),
            vmem((ny, side, SLAB), BF16),
            vmem((ny, side, SLAB), BF16),
            vmem((ny, side, SLAB), BF16),
            vmem((ny, side, SLAB), BF16),
            vmem((nm, ROWS, SLAB), F32),
            vmem((nm, ROWS, SLAB), F32),
            vmem((TILE, TILE), F32),
            vmem((TILE, TILE), F32),
            many((7,)),
            many((no,)),
            many((no,)),
            many,
            many,
            many((nm,)),
            many((nm,)),
            many((no,)),
            many((no,)),
            many((nz,)),
            many((nz,)),
            many((NX,)),
            many((NX,)),
            many((nz,)),
            many((nz,)),
            many((NX,)),
            many((NX,)),
            many((NX,)),
            many((NX,)),
            many((ny,)),
            many((ny,)),
            many((ny,)),
            many((ny,)),
            many((nm,)),
            many((nm,)),
        ],
        compiler_params=pltpu.CompilerParams(
            collective_id=0, has_side_effects=True, vmem_limit_bytes=60 * 1024 * 1024
        ),
    )(members, alphas, points, labels.reshape(1, TILE), noise.reshape(1, TILE), observed.reshape(1, TILE), perturb)


def solution(mesh):
    in_specs = (P(("mem", "obs"), None), P(), P(), P("obs"), P("obs"), P("obs"), P("mem", "obs"))
    out_specs = P(("mem", "obs"), None)
    return jax.shard_map(shards, mesh=mesh, in_specs=in_specs, out_specs=out_specs, check_vma=False)
```

time: 67.4 us -> 57.5 us (0.85)
  Pallas kernels: 62.5 us -> 55.8 us
  local copies, waits for them, and re-layouts: 4.56 us -> 1.57 us
    pallas_call x1, Pallas kernels: 62.5 us -> 55.8 us  [shards(): pl.pallas_call(lambda *refs: kernel(nm, no, *refs), out_shape=jax.ShapeDt...]
    unnamed x15 -> x1, local copies, waits for them, and re-layouts: 4.56 us -> 1.57 us
where the time goes in v2:
time: 57.5 us; the launch traced here: 57.4 us
  Pallas kernels  55.8 us (97%)
  local copies, waits for them, and re-layouts  1.57 us (3%)
    pallas_call x1, Pallas kernels, shards(): pl.pallas_call(lambda *refs: kernel(nm, no, *refs), out_shape=jax.ShapeDt...  55.8 us
    unnamed x1, local copies, waits for them, and re-layouts  1.57 us

profile of v2, /device:TPU:1, one launch (start us, length us, event | category | flops | bytes accessed | tf_op | source)
XLA Modules:
  0.0 57.4 jit_solution(403683262301167196)
XLA Ops:
  0.0 55.8 %shard_map.73 = f32[8,4096]{1,0:T(8,128)} custom-call(bf16[8,4096]{1,0:T(8,128)(2,1)} %refs_0_.1, s32[8,4096]{1,0:T(8,128)} %refs_1_.1, f32[8,1024]{1,0:T(8,128)} %refs_2_.1, s32[1,128]{1,0:T(1,128)} %bitcast.3, f32[1,128]{1,0:T(1,128)} %bitcast.4, f32[1,128]{1,0:T(1,128)} %bitcast.5, bf16[64,128]{1,0:T(8,128)(2,1)} %refs_6_.1), custom_call_target="tpu_custom_call" | custom-call | tf_op jit(solution)/shard_map/pallas_call | solution.py:462
  55.8 1.6 %copy.9 = f32[8,4096]{1,0:T(8,128)} copy(f32[8,4096]{1,0:T(8,128)} %shard_map.73) | data formatting | bytes 262144

commit v3 on v2

v3 whole, which is shorter than its diff:
```python
import math

import jax
import jax.numpy as jnp
from jax import lax
from jax.experimental import pallas as pl
from jax.experimental.pallas import tpu as pltpu
from jax.sharding import PartitionSpec as P

ROWS = 8
TILE = 128
SLAB = 128
PANEL = 8
CHUNK = 256
NX = 4
F32 = jnp.float32
BF16 = jnp.bfloat16
FIRST = (((0,), (0,)), ((), ()))
LAST = (((1,), (1,)), ((), ()))
PLAIN = (((1,), (0,)), ((), ()))


def dot(left, right, dims, precision=None):
    return lax.dot_general(left, right, dims, precision=precision, preferred_element_type=F32)


def inverse_blocks(matrix, first, last):
    size = matrix.shape[0]
    row = lax.broadcasted_iota(jnp.int32, (PANEL, size), 0)
    lane = lax.broadcasted_iota(jnp.int32, (PANEL, size), 1)
    rest_lane = lax.broadcasted_iota(jnp.int32, (size - PANEL, size), 1)
    unit = jnp.where(lane == row, 1.0, 0.0).astype(F32)

    def block(_, full):
        top, rest = full[:PANEL], full[PANEL:]
        column = [jnp.broadcast_to(top[:, j : j + 1], (PANEL, size)) for j in range(PANEL)]
        panel = jnp.where(lane < PANEL, unit, top)
        for p in range(PANEL):
            scale = 1.0 / column[p][p : p + 1]
            pivot = panel[p : p + 1] * scale
            panel = jnp.where(row == p, pivot, panel - column[p] * pivot)
            for j in range(p + 1, PANEL):
                entry = column[j][p : p + 1] * scale
                column[j] = jnp.where(row == p, entry, column[j] - column[p] * entry)
        update = jnp.where(rest_lane < PANEL, 0.0, rest)
        for j in range(PANEL):
            update = update - rest[:, j : j + 1] * panel[j : j + 1]
        return pltpu.roll(jnp.concatenate([update, panel], axis=0), size - PANEL, 1)

    return lax.fori_loop(first, last, block, matrix)


def kernel(
    nm,
    no,
    members_hbm,
    alphas_hbm,
    points_hbm,
    labels_hbm,
    noise_hbm,
    observed_hbm,
    perturb_hbm,
    out,
    members,
    alphas,
    points,
    labels,
    noise,
    observed,
    rows_out,
    rows_in,
    halves,
    half_in,
    blocks_out,
    blocks_in,
    slabs,
    preds,
    perts,
    grams,
    table,
    basis,
    innov,
    prior,
    cross_out,
    cross_in,
    crosses,
    mine,
    pair_out,
    pair_in,
    share_out,
    share_in,
    incr_out,
    final,
    coupled,
    spread,
    right_r,
    left_r,
    local_s,
    rows_s,
    rows_r,
    half_s,
    half_r,
    blocks_s,
    blocks_r,
    slabs_s,
    slabs_r,
    preds_s,
    preds_r,
    perts_s,
    perts_r,
    grams_s,
    grams_r,
    cross_s,
    cross_r,
    crosses_s,
    crosses_r,
    pair_s,
    pair_r,
    share_s,
    share_r,
    incr_s,
    incr_r,
):
    g, o = lax.axis_index("mem"), lax.axis_index("obs")
    z, x = lax.div(g, NX), lax.rem(g, NX)
    y, c = lax.div(o, 2), lax.rem(o, 2)
    nz, ny = nm // NX, no // 2
    coeffs = members.shape[1]
    half = coeffs // 2
    quarter = half // 2
    width = coeffs // nz
    chunk = min(CHUNK, quarter)
    ensemble = nm * no * ROWS
    line = nz * no * ROWS
    side = nz * ROWS
    mesh = pl.DeviceIdType.MESH

    def obs_at(d):
        return lax.rem(o + d, no)

    def z_at(d):
        return lax.rem(z + d, nz)

    def x_at(d):
        return lax.rem(x + d, NX)

    def y_at(d):
        return lax.rem(y + d, ny)

    def in_z(at):
        return (at * NX + x, o)

    def in_x(at):
        return (z * NX + at, o)

    sibling = y * 2 + 1 - c

    def copy(src, dst, send, recv, to):
        return pltpu.make_async_remote_copy(
            src_ref=src, dst_ref=dst, send_sem=send, recv_sem=recv, device_id=to, device_id_type=mesh
        )

    def tell(semaphore, to):
        pl.semaphore_signal(semaphore, inc=1, device_id=to, device_id_type=mesh)

    def each(count, act):
        def step(d, carry):
            act(d)
            return carry

        lax.fori_loop(1, count, step, 0)

    fetch = [
        pltpu.make_async_copy(src, dst, local_s.at[k])
        for k, (src, dst) in enumerate(
            (
                (members_hbm, members),
                (points_hbm.at[:, pl.ds(pl.multiple_of(y * 2 * TILE, 2 * TILE), 2 * TILE)], points),
                (labels_hbm, labels),
                (noise_hbm, noise),
                (observed_hbm, observed),
                (perturb_hbm, perts.at[z]),
                (alphas_hbm, alphas),
            )
        )
    ]
    for f in fetch:
        f.start()

    barrier = pltpu.get_barrier_semaphore()
    after, before = z_at(1), z_at(nz - 1)
    each(no, lambda d: tell(barrier, (g, obs_at(d))))
    each(NX, lambda d: tell(barrier, in_x(x_at(d))))
    tell(barrier, in_z(after))
    tell(barrier, in_z(before))

    fetch[0].wait()
    own = members[...].astype(F32)
    for h in range(2):
        part = own[:, h * half : (h + 1) * half]
        rows_out[h] = jnp.concatenate([part[:, :quarter], part[:, quarter:]], axis=0).astype(BF16)
    rows_in[o] = rows_out[c]
    for k in range(nz):
        part = own[:, k * width : (k + 1) * width]
        blocks_out[k] = jnp.concatenate([part[:, : width // 2], part[:, width // 2 :]], axis=0).astype(BF16)
    blocks_in[z] = blocks_out[z]

    fetch[1].wait()
    for t in range(2):
        at = points[:, t * TILE : (t + 1) * TILE]
        turned = jnp.concatenate([at, jnp.zeros((TILE - at.shape[0], TILE), F32)], axis=0).T
        for d in range(at.shape[0]):
            value = jnp.broadcast_to(turned[:, d : d + 1], (TILE, TILE))
            second = value * value - 1.0
            third = value * second - 2.0 * value
            table[t, d, 0] = value
            table[t, d, 1] = second * (1.0 / math.sqrt(2.0))
            table[t, d, 2] = third * (1.0 / math.sqrt(6.0))

    pl.semaphore_wait(barrier, no - 1 + NX - 1 + 2)

    def rows_to(d):
        to = obs_at(d)
        return copy(rows_out.at[lax.rem(to, 2)], rows_in.at[o], rows_s.at[d], rows_r.at[o], (g, to))

    def rows_from(d):
        at = obs_at(d)
        return copy(rows_out.at[c], rows_in.at[at], rows_s.at[d], rows_r.at[at], (g, at))

    each(no, lambda d: rows_to(d).start())

    for f in fetch[2:]:
        f.wait()
    label = jnp.broadcast_to(labels[...].astype(F32), (TILE, TILE))
    diagonal = lax.broadcasted_iota(jnp.int32, (TILE, TILE), 0) == lax.broadcasted_iota(jnp.int32, (TILE, TILE), 1)
    coupled[...] = jnp.where(label == label.T, 1.0 / (ensemble - 1), 0.0).astype(F32)
    spread[...] = jnp.where(diagonal, jnp.broadcast_to(noise[...], (TILE, TILE)), 0.0)

    def basis_part(first_step, last_step):
        def step(n, carry):
            per = quarter // chunk
            q, t, k = lax.div(n, 2 * per), lax.rem(lax.div(n, per), 2), lax.rem(n, per)
            first = pl.multiple_of(k * chunk, chunk)
            degree = alphas[:, pl.ds(pl.multiple_of(c * half + q * quarter + first, chunk), chunk)]
            product = None
            for d in range(degree.shape[0]):
                odd = (degree[d : d + 1] & 1) == 1
                high = degree[d : d + 1] >= 2
                one, two, three = (jnp.concatenate([table[t, d, p]] * (chunk // TILE), axis=1) for p in range(3))
                value = jnp.where(high, jnp.where(odd, three, two), jnp.where(odd, one, 1.0))
                product = value if product is None else product * value
            place = pl.multiple_of((q * 2 + t) * TILE, TILE)
            basis[pl.ds(place, TILE), pl.ds(first, chunk)] = product.astype(BF16)
            return carry

        lax.fori_loop(first_step, last_step, step, 0)

    steps = 4 * (quarter // chunk)
    stages = nz // 2 - 1
    for k in range(stages):
        tell(right_r.at[k], in_z(after))
        tell(left_r.at[k], in_z(before))
        basis_part(steps * k // (stages + 1), steps * (k + 1) // (stages + 1))
        pl.semaphore_wait(right_r.at[k], 1)
        pl.semaphore_wait(left_r.at[k], 1)

    def block_to(d):
        return copy(blocks_out.at[z_at(d)], blocks_in.at[z], blocks_s.at[d], blocks_r.at[z], in_z(z_at(d)))

    def block_from(d):
        at = z_at(d)
        return copy(blocks_out.at[at], blocks_in.at[at], blocks_s.at[d], blocks_r.at[at], in_z(at))

    def pert_to(d):
        return copy(perts.at[z], perts.at[z], perts_s.at[d], perts_r.at[z], in_z(z_at(d)))

    def pert_from(d):
        at = z_at(d)
        return copy(perts.at[at], perts.at[at], perts_s.at[d], perts_r.at[at], in_z(at))

    each(nz, lambda d: block_to(d).start())
    each(nz, lambda d: pert_to(d).start())
    basis_part(steps * stages // (stages + 1), steps)

    each(no, lambda d: rows_from(d).wait_recv())
    both = dot(rows_in[...].reshape(no * 2 * ROWS, quarter), basis[...], LAST)
    both = both.reshape(no, 2, ROWS, 4 * TILE)
    part = (both[:, 0, :, : 2 * TILE] + both[:, 1, :, 2 * TILE :]).reshape(no * ROWS, 2 * TILE)
    for t in range(2):
        halves[t] = part[:, t * TILE : (t + 1) * TILE]
    half_copy = copy(halves.at[1 - c], half_in, half_s, half_r, (g, sibling))
    half_copy.start()
    half_copy.wait_recv()
    preds[z] = (halves[c] + half_in[...]).astype(BF16)

    def pred_to(d):
        return copy(preds.at[z], preds.at[z], preds_s.at[d], preds_r.at[z], in_z(z_at(d)))

    def pred_from(d):
        at = z_at(d)
        return copy(preds.at[at], preds.at[at], preds_s.at[d], preds_r.at[at], in_z(at))

    each(nz, lambda d: pred_to(d).start())

    each(nz, lambda d: block_from(d).wait_recv())
    block = blocks_in[...].astype(F32)
    block = jnp.concatenate([block[:, :ROWS], block[:, ROWS:]], axis=2)
    slabs[o] = block.reshape(side, width).astype(BF16)

    def slab_to(d):
        return copy(slabs.at[o], slabs.at[o], slabs_s.at[d], slabs_r.at[o], (g, y_at(d) * 2 + c))

    def slab_from(at, to):
        return copy(slabs.at[at], slabs.at[at], slabs_s.at[0], slabs_r.at[at], (g, to))

    def slab_pass(d):
        at = y_at(d) * 2 + c
        return copy(slabs.at[at], slabs.at[at], slabs_s.at[ny + d], slabs_r.at[at], (g, sibling))

    slab_own = copy(slabs.at[o], slabs.at[o], slabs_s.at[0], slabs_r.at[o], (g, sibling))
    each(ny, lambda d: slab_to(d).start())
    slab_own.start()

    each(nz, lambda d: pred_from(d).wait_recv())
    flat = preds[...].reshape(line, TILE)
    ones = jnp.ones((2 * ROWS, line), BF16)
    grams[x, :TILE] = dot(flat, flat, FIRST)
    grams[x, TILE:] = dot(ones, flat, PLAIN)[:ROWS]

    def gram_to(d):
        return copy(grams.at[x], grams.at[x], grams_s.at[d], grams_r.at[x], in_x(x_at(d)))

    def gram_from(d):
        at = x_at(d)
        return copy(grams.at[at], grams.at[at], grams_s.at[d], grams_r.at[at], in_x(at))

    each(NX, lambda d: gram_to(d).start())

    def pass_on(d):
        at = y_at(d) * 2 + c
        slab_from(at, at).wait_recv()
        slab_pass(d).start()

    each(ny, pass_on)

    each(nz, lambda d: pert_from(d).wait_recv())
    noise_root = jnp.sqrt(noise[...])
    for t in range(nz):
        value = preds[t].astype(F32)
        left = observed[...] + noise_root * perts[t].astype(F32) - value
        for k in range(no):
            prior[k, t * ROWS : (t + 1) * ROWS, :] = value[k * ROWS : (k + 1) * ROWS]
            innov[k % 2, k // 2, t * ROWS : (t + 1) * ROWS, :] = left[k * ROWS : (k + 1) * ROWS]
    ordered = prior[...].reshape(line, TILE).astype(BF16)

    slab_from(sibling, sibling).wait_recv()
    each(ny, lambda d: slab_from(y_at(d) * 2 + 1 - c, sibling).wait_recv())
    slab = slabs[...].reshape(line, width)
    raw = dot(ordered, slab, FIRST)
    total = dot(ones, slab, PLAIN)[:ROWS]
    for k in range(NX):
        cross_out[k, :TILE] = raw[:, k * SLAB : (k + 1) * SLAB]
        cross_out[k, TILE:] = total[:, k * SLAB : (k + 1) * SLAB]
    cross_in[x] = cross_out[x]

    def cross_to(d):
        at = x_at(d)
        return copy(cross_out.at[at], cross_in.at[x], cross_s.at[d], cross_r.at[x], in_x(at))

    def cross_from(d):
        at = x_at(d)
        return copy(cross_out.at[at], cross_in.at[at], cross_s.at[d], cross_r.at[at], in_x(at))

    each(NX, lambda d: cross_to(d).start())

    each(NX, lambda d: gram_from(d).wait_recv())
    gram = grams[0]
    for k in range(1, NX):
        gram = gram + grams[k]
    mean_pred = jnp.broadcast_to(gram[TILE : TILE + 1] / ensemble, (TILE, TILE))
    mean_turned = mean_pred.T
    system = (gram[:TILE] - ensemble * mean_turned * mean_pred) * coupled[...] + spread[...]

    inverted = inverse_blocks(system, 0, TILE // PANEL // 2)

    each(NX, lambda d: cross_from(d).wait_recv())
    cross = cross_in[0]
    for k in range(1, NX):
        cross = cross + cross_in[k]
    mean_param = cross[TILE : TILE + 1] / ensemble
    crosses[x] = cross[:TILE] - ensemble * mean_turned * mean_param

    def crosses_to(d):
        return copy(crosses.at[x], crosses.at[x], crosses_s.at[d], crosses_r.at[x], in_x(x_at(d)))

    def crosses_from(d):
        at = x_at(d)
        return copy(crosses.at[at], crosses.at[at], crosses_s.at[d], crosses_r.at[at], in_x(at))

    each(NX, lambda d: crosses_to(d).start())

    inverted = inverse_blocks(inverted, TILE // PANEL // 2, TILE // PANEL)

    each(NX, lambda d: crosses_from(d).wait_recv())
    cross = jnp.concatenate([crosses[k] for k in range(NX)], axis=1)
    gain = dot(inverted, cross, PLAIN, lax.Precision.HIGHEST) / (ensemble - 1)
    high = gain.astype(BF16)
    low = (gain - high.astype(F32)).astype(BF16)
    weights = jnp.concatenate([high, low], axis=1)
    weights = jnp.concatenate([weights, weights], axis=0)

    def share(core):
        left = innov[core].reshape(ny * side, TILE)
        big = left.astype(BF16)
        small = (left - big.astype(F32)).astype(BF16)
        parts = dot(jnp.concatenate([big, small], axis=1), weights, PLAIN)
        return (parts[:, :width] + parts[:, width:]).reshape(ny, side, width)

    def pair_copy(d):
        at = y_at(d)
        return copy(pair_out.at[at], pair_in.at[at], pair_s.at[at], pair_r.at[at], (g, sibling))

    def share_to(d):
        at = y_at(d)
        return copy(share_out.at[at], share_in.at[y], share_s.at[d], share_r.at[y], (g, at * 2 + c))

    def share_from(d):
        at = y_at(d)
        return copy(share_out.at[at], share_in.at[at], share_s.at[d], share_r.at[at], (g, at * 2 + c))

    turns = sorted(range(1, ny), key=lambda d: -min(d, ny - d)) + [0]
    pair_out[...] = share(1 - c).astype(BF16)
    for d in turns:
        pair_copy(d).start()
    mine[...] = share(c)
    for d in turns:
        at = y_at(d)
        pair_copy(d).wait_recv()
        total = mine[at] + pair_in[at].astype(F32)
        if d:
            share_out[at] = total.astype(BF16)
            share_to(d).start()
    for d in turns[:-1]:
        share_from(d).wait_recv()
        total = total + share_in[y_at(d)].astype(F32)
    incr_out[...] = total.reshape(nz, ROWS, width)

    def incr_to(d):
        at = z_at(d)
        return copy(incr_out.at[at], final.at[z], incr_s.at[d], incr_r.at[z], in_z(at))

    def incr_from(d):
        at = z_at(d)
        return copy(incr_out.at[at], final.at[at], incr_s.at[d], incr_r.at[at], in_z(at))

    each(nz, lambda d: incr_to(d).start())
    final[z] = incr_out[z]
    each(nz, lambda d: incr_from(d).wait_recv())
    for k in range(nz):
        at = slice(k * width, (k + 1) * width)
        out[:, at] = members[:, at].astype(F32) + final[k]

    def obs_sent(d):
        rows_to(d).wait_send()

    def y_sent(d):
        slab_to(d).wait_send()
        slab_pass(d).wait_send()
        share_to(d).wait_send()
        pair_copy(d).wait_send()

    def z_sent(d):
        block_to(d).wait_send()
        pert_to(d).wait_send()
        pred_to(d).wait_send()
        incr_to(d).wait_send()

    def x_sent(d):
        gram_to(d).wait_send()
        cross_to(d).wait_send()
        crosses_to(d).wait_send()

    half_copy.wait_send()
    slab_own.wait_send()
    pair_copy(0).wait_send()
    each(no, obs_sent)
    each(ny, y_sent)
    each(nz, z_sent)
    each(NX, x_sent)


def shards(members, alphas, points, labels, noise, observed, perturb):
    nm, no = lax.axis_size("mem"), lax.axis_size("obs")
    nz, ny = nm // NX, no // 2
    coeffs = members.shape[1]
    dims = alphas.shape[0]
    side, width = nz * ROWS, coeffs // nz
    vmem, many = pltpu.VMEM, pltpu.SemaphoreType.DMA
    signal = pltpu.SemaphoreType.REGULAR
    stages = nz // 2 - 1
    return pl.pallas_call(
        lambda *refs: kernel(nm, no, *refs),
        out_shape=jax.ShapeDtypeStruct((ROWS, coeffs), F32),
        in_specs=[pl.BlockSpec(memory_space=pl.ANY)] * 7,
        out_specs=pl.BlockSpec(memory_space=vmem),
        scratch_shapes=[
            vmem((ROWS, coeffs), BF16),
            vmem((dims, coeffs), jnp.int32),
            vmem((dims, 2 * TILE), F32),
            vmem((1, TILE), jnp.int32),
            vmem((1, TILE), F32),
            vmem((1, TILE), F32),
            vmem((2, 2 * ROWS, coeffs // 4), BF16),
            vmem((no, 2 * ROWS, coeffs // 4), BF16),
            vmem((2, no * ROWS, TILE), F32),
            vmem((no * ROWS, TILE), F32),
            vmem((nz, 2 * ROWS, width // 2), BF16),
            vmem((nz, 2 * ROWS, width // 2), BF16),
            vmem((no, side, width), BF16),
            vmem((nz, no * ROWS, TILE), BF16),
            vmem((nz, no * ROWS, TILE), BF16),
            vmem((NX, TILE + ROWS, TILE), F32),
            vmem((2, dims, 3, TILE, TILE), F32),
            vmem((4 * TILE, coeffs // 4), BF16),
            vmem((2, ny, side, TILE), F32),
            vmem((no, side, TILE), F32),
            vmem((NX, TILE + ROWS, SLAB), F32),
            vmem((NX, TILE + ROWS, SLAB), F32),
            vmem((NX, TILE, SLAB), F32),
            vmem((ny, side, width), F32),
            vmem((ny, side, width), BF16),
            vmem((ny, side, width), BF16),
            vmem((ny, side, width), BF16),
            vmem((ny, side, width), BF16),
            vmem((nz, ROWS, width), F32),
            vmem((nz, ROWS, width), F32),
            vmem((TILE, TILE), F32),
            vmem((TILE, TILE), F32),
            signal((stages,)),
            signal((stages,)),
            many((7,)),
            many((no,)),
            many((no,)),
            many,
            many,
            many((nz,)),
            many((nz,)),
            many((no,)),
            many((no,)),
            many((nz,)),
            many((nz,)),
            many((nz,)),
            many((nz,)),
            many((NX,)),
            many((NX,)),
            many((NX,)),
            many((NX,)),
            many((NX,)),
            many((NX,)),
            many((ny,)),
            many((ny,)),
            many((ny,)),
            many((ny,)),
            many((nz,)),
            many((nz,)),
        ],
        compiler_params=pltpu.CompilerParams(
            collective_id=0, has_side_effects=True, vmem_limit_bytes=60 * 1024 * 1024
        ),
    )(members, alphas, points, labels.reshape(1, TILE), noise.reshape(1, TILE), observed.reshape(1, TILE), perturb)


def solution(mesh):
    in_specs = (P(("mem", "obs"), None), P(), P(), P("obs"), P("obs"), P("obs"), P("mem", "obs"))
    out_specs = P(("mem", "obs"), None)
    return jax.shard_map(shards, mesh=mesh, in_specs=in_specs, out_specs=out_specs, check_vma=False)
```

time: 57.5 us -> 54 us (0.939)
  Pallas kernels: 55.8 us -> 52.3 us
    pallas_call x1, Pallas kernels: 55.8 us -> 52.3 us  [shards(): pl.pallas_call(lambda *refs: kernel(nm, no, *refs), out_shape=jax.ShapeDt...]
where the time goes in v3:
time: 54 us; the launch traced here: 53.8 us
  Pallas kernels  52.3 us (97%)
  local copies, waits for them, and re-layouts  1.57 us (3%)
    pallas_call x1, Pallas kernels, shards(): pl.pallas_call(lambda *refs: kernel(nm, no, *refs), out_shape=jax.ShapeDt...  52.3 us
    unnamed x1, local copies, waits for them, and re-layouts  1.57 us

profile of v3, /device:TPU:1, one launch (start us, length us, event | category | flops | bytes accessed | tf_op | source)
XLA Modules:
  0.0 53.8 jit_solution(13760742768485965049)
XLA Ops:
  0.0 52.3 %shard_map.73 = f32[8,4096]{1,0:T(8,128)} custom-call(bf16[8,4096]{1,0:T(8,128)(2,1)} %refs_0_.1, s32[8,4096]{1,0:T(8,128)} %refs_1_.1, f32[8,1024]{1,0:T(8,128)} %refs_2_.1, s32[1,128]{1,0:T(1,128)} %bitcast.3, f32[1,128]{1,0:T(1,128)} %bitcast.4, f32[1,128]{1,0:T(1,128)} %bitcast.5, bf16[64,128]{1,0:T(8,128)(2,1)} %refs_6_.1), custom_call_target="tpu_custom_call" | custom-call | tf_op jit(solution)/shard_map/pallas_call | solution.py:501
  52.3 1.6 %copy.9 = f32[8,4096]{1,0:T(8,128)} copy(f32[8,4096]{1,0:T(8,128)} %shard_map.73) | data formatting | bytes 262144

commit v4 on v3

--- a/solution.py
+++ b/solution.py
@@ -48,6 +48,32 @@
         return pltpu.roll(jnp.concatenate([update, panel], axis=0), size - PANEL, 1)
 
     return lax.fori_loop(first, last, block, matrix)
+
+
+def places(rows):
+    shape = (rows, TILE)
+    return lax.broadcasted_iota(jnp.int32, shape, 0), lax.broadcasted_iota(jnp.int32, shape, 1)
+
+
+def folded(square):
+    edge = TILE // 2
+    row, lane = places(edge)
+    return jnp.where(lane >= row, square[:edge], pltpu.roll(square[edge:], edge, 1))
+
+
+def diagonal_row(square):
+    row, lane = places(TILE)
+    kept = jnp.sum(jnp.where(row == lane, square, 0.0), axis=0, keepdims=True)
+    return jnp.broadcast_to(kept, (ROWS, TILE))
+
+
+def unfolded(half, kept):
+    edge = TILE // 2
+    row, lane = places(TILE)
+    whole = jnp.concatenate([half, pltpu.roll(half, edge, 1)], axis=0)
+    direct = jnp.where(row < edge, lane - row, jnp.where(lane >= edge, row - lane - 1, -1)) >= 0
+    square = jnp.where(direct, whole, whole.T)
+    return jnp.where((row == lane) & (row >= edge), jnp.broadcast_to(kept[:1], (TILE, TILE)), square)
 
 
 def kernel(
@@ -84,7 +110,6 @@
     cross_out,
     cross_in,
     crosses,
-    mine,
     pair_out,
     pair_in,
     share_out,
@@ -93,8 +118,7 @@
     final,
     coupled,
     spread,
-    right_r,
-    left_r,
+    ready,
     local_s,
     rows_s,
     rows_r,
@@ -170,6 +194,12 @@
 
         lax.fori_loop(1, count, step, 0)
 
+    far = sorted(range(1, nz), key=lambda d: -min(d, nz - d))
+
+    turns_z = far + [0]
+    turns = sorted(range(1, ny), key=lambda d: -min(d, ny - d)) + [0]
+    fore = side // 2
+
     fetch = [
         pltpu.make_async_copy(src, dst, local_s.at[k])
         for k, (src, dst) in enumerate(
@@ -188,11 +218,12 @@
         f.start()
 
     barrier = pltpu.get_barrier_semaphore()
-    after, before = z_at(1), z_at(nz - 1)
+    reach = range(1, nz // 4 + 1)
+    near = [in_z(z_at(s * k % nz)) for k in reach for s in (1, -1)]
     each(no, lambda d: tell(barrier, (g, obs_at(d))))
     each(NX, lambda d: tell(barrier, in_x(x_at(d))))
-    tell(barrier, in_z(after))
-    tell(barrier, in_z(before))
+    for to in near:
+        tell(barrier, to)
 
     fetch[0].wait()
     own = members[...].astype(F32)
@@ -205,8 +236,24 @@
         blocks_out[k] = jnp.concatenate([part[:, : width // 2], part[:, width // 2 :]], axis=0).astype(BF16)
     blocks_in[z] = blocks_out[z]
 
+    pl.semaphore_wait(barrier, no - 1 + NX - 1 + len(near))
+
+    def rows_to(d):
+        to = obs_at(d)
+        return copy(rows_out.at[lax.rem(to, 2)], rows_in.at[o], rows_s.at[d], rows_r.at[o], (g, to))
+
+    def rows_from(d):
+        at = obs_at(d)
+        return copy(rows_out.at[c], rows_in.at[at], rows_s.at[d], rows_r.at[at], (g, at))
+
+    for d in sorted(range(1, no), key=lambda d: -min(d, no - d)):
+        rows_to(d).start()
+    for to in near[-2:]:
+        tell(ready, to)
+
     fetch[1].wait()
-    for t in range(2):
+
+    def tabulate(t):
         at = points[:, t * TILE : (t + 1) * TILE]
         turned = jnp.concatenate([at, jnp.zeros((TILE - at.shape[0], TILE), F32)], axis=0).T
         for d in range(at.shape[0]):
@@ -217,17 +264,8 @@
             table[t, d, 1] = second * (1.0 / math.sqrt(2.0))
             table[t, d, 2] = third * (1.0 / math.sqrt(6.0))
 
-    pl.semaphore_wait(barrier, no - 1 + NX - 1 + 2)
-
-    def rows_to(d):
-        to = obs_at(d)
-        return copy(rows_out.at[lax.rem(to, 2)], rows_in.at[o], rows_s.at[d], rows_r.at[o], (g, to))
-
-    def rows_from(d):
-        at = obs_at(d)
-        return copy(rows_out.at[c], rows_in.at[at], rows_s.at[d], rows_r.at[at], (g, at))
-
-    each(no, lambda d: rows_to(d).start())
+    tabulate(0)
+    tabulate(1)
 
     for f in fetch[2:]:
         f.wait()
@@ -256,13 +294,8 @@
         lax.fori_loop(first_step, last_step, step, 0)
 
     steps = 4 * (quarter // chunk)
-    stages = nz // 2 - 1
-    for k in range(stages):
-        tell(right_r.at[k], in_z(after))
-        tell(left_r.at[k], in_z(before))
-        basis_part(steps * k // (stages + 1), steps * (k + 1) // (stages + 1))
-        pl.semaphore_wait(right_r.at[k], 1)
-        pl.semaphore_wait(left_r.at[k], 1)
+    basis_part(0, steps // 8)
+    pl.semaphore_wait(ready, 2)
 
     def block_to(d):
         return copy(blocks_out.at[z_at(d)], blocks_in.at[z], blocks_s.at[d], blocks_r.at[z], in_z(z_at(d)))
@@ -278,9 +311,9 @@
         at = z_at(d)
         return copy(perts.at[at], perts.at[at], perts_s.at[d], perts_r.at[at], in_z(at))
 
-    each(nz, lambda d: block_to(d).start())
-    each(nz, lambda d: pert_to(d).start())
-    basis_part(steps * stages // (stages + 1), steps)
+    for d in far:
+        block_to(d).start()
+    basis_part(steps // 8, steps)
 
     each(no, lambda d: rows_from(d).wait_recv())
     both = dot(rows_in[...].reshape(no * 2 * ROWS, quarter), basis[...], LAST)
@@ -300,7 +333,8 @@
         at = z_at(d)
         return copy(preds.at[at], preds.at[at], preds_s.at[d], preds_r.at[at], in_z(at))
 
-    each(nz, lambda d: pred_to(d).start())
+    for d in far:
+        pred_to(d).start()
 
     each(nz, lambda d: block_from(d).wait_recv())
     block = blocks_in[...].astype(F32)
@@ -321,21 +355,6 @@
     each(ny, lambda d: slab_to(d).start())
     slab_own.start()
 
-    each(nz, lambda d: pred_from(d).wait_recv())
-    flat = preds[...].reshape(line, TILE)
-    ones = jnp.ones((2 * ROWS, line), BF16)
-    grams[x, :TILE] = dot(flat, flat, FIRST)
-    grams[x, TILE:] = dot(ones, flat, PLAIN)[:ROWS]
-
-    def gram_to(d):
-        return copy(grams.at[x], grams.at[x], grams_s.at[d], grams_r.at[x], in_x(x_at(d)))
-
-    def gram_from(d):
-        at = x_at(d)
-        return copy(grams.at[at], grams.at[at], grams_s.at[d], grams_r.at[at], in_x(at))
-
-    each(NX, lambda d: gram_to(d).start())
-
     def pass_on(d):
         at = y_at(d) * 2 + c
         slab_from(at, at).wait_recv()
@@ -343,14 +362,27 @@
 
     each(ny, pass_on)
 
-    each(nz, lambda d: pert_from(d).wait_recv())
-    noise_root = jnp.sqrt(noise[...])
+    each(nz, lambda d: pred_from(d).wait_recv())
+    flat = preds[...].reshape(line, TILE)
+    ones = jnp.ones((2 * ROWS, line), BF16)
+    gram = dot(flat, flat, FIRST)
+    grams[x] = jnp.concatenate([folded(gram), dot(ones, flat, PLAIN)[:ROWS], diagonal_row(gram)], axis=0)
+
+    def gram_to(d):
+        return copy(grams.at[x], grams.at[x], grams_s.at[d], grams_r.at[x], in_x(x_at(d)))
+
+    def gram_from(d):
+        at = x_at(d)
+        return copy(grams.at[at], grams.at[at], grams_s.at[d], grams_r.at[at], in_x(at))
+
+    each(NX, lambda d: gram_to(d).start())
+    for d in far:
+        pert_to(d).start()
+
     for t in range(nz):
         value = preds[t].astype(F32)
-        left = observed[...] + noise_root * perts[t].astype(F32) - value
         for k in range(no):
             prior[k, t * ROWS : (t + 1) * ROWS, :] = value[k * ROWS : (k + 1) * ROWS]
-            innov[k % 2, k // 2, t * ROWS : (t + 1) * ROWS, :] = left[k * ROWS : (k + 1) * ROWS]
     ordered = prior[...].reshape(line, TILE).astype(BF16)
 
     slab_from(sibling, sibling).wait_recv()
@@ -377,9 +409,10 @@
     gram = grams[0]
     for k in range(1, NX):
         gram = gram + grams[k]
-    mean_pred = jnp.broadcast_to(gram[TILE : TILE + 1] / ensemble, (TILE, TILE))
+    mean_pred = jnp.broadcast_to(gram[TILE // 2 : TILE // 2 + 1] / ensemble, (TILE, TILE))
     mean_turned = mean_pred.T
-    system = (gram[:TILE] - ensemble * mean_turned * mean_pred) * coupled[...] + spread[...]
+    gram = unfolded(gram[: TILE // 2], gram[TILE // 2 + ROWS :])
+    system = (gram - ensemble * mean_turned * mean_pred) * coupled[...] + spread[...]
 
     inverted = inverse_blocks(system, 0, TILE // PANEL // 2)
 
@@ -398,6 +431,14 @@
         return copy(crosses.at[at], crosses.at[at], crosses_s.at[d], crosses_r.at[at], in_x(at))
 
     each(NX, lambda d: crosses_to(d).start())
+
+    each(nz, lambda d: pert_from(d).wait_recv())
+    noise_root = jnp.sqrt(noise[...])
+    for t, d in enumerate(turns_z):
+        at = z_at(d)
+        left = observed[...] + noise_root * perts[at].astype(F32) - preds[at].astype(F32)
+        for k in range(no):
+            innov[k % 2, k // 2, t * ROWS : (t + 1) * ROWS, :] = left[k * ROWS : (k + 1) * ROWS]
 
     inverted = inverse_blocks(inverted, TILE // PANEL // 2, TILE // PANEL)
 
@@ -409,83 +450,87 @@
     weights = jnp.concatenate([high, low], axis=1)
     weights = jnp.concatenate([weights, weights], axis=0)
 
-    def share(core):
-        left = innov[core].reshape(ny * side, TILE)
+    def share(core, d):
+        left = innov[core, y_at(d)]
         big = left.astype(BF16)
         small = (left - big.astype(F32)).astype(BF16)
         parts = dot(jnp.concatenate([big, small], axis=1), weights, PLAIN)
-        return (parts[:, :width] + parts[:, width:]).reshape(ny, side, width)
+        return parts[:, :width] + parts[:, width:]
 
     def pair_copy(d):
+        return copy(pair_out.at[d], pair_in.at[d], pair_s.at[d], pair_r.at[d], (g, sibling))
+
+    def share_to(d, h):
+        span = pl.ds(h * fore, fore)
+        to = (g, y_at(d) * 2 + c)
+        return copy(share_out.at[d, span], share_in.at[y, span], share_s.at[d, h], share_r.at[y, h], to)
+
+    def share_from(d, h):
         at = y_at(d)
-        return copy(pair_out.at[at], pair_in.at[at], pair_s.at[at], pair_r.at[at], (g, sibling))
-
-    def share_to(d):
-        at = y_at(d)
-        return copy(share_out.at[at], share_in.at[y], share_s.at[d], share_r.at[y], (g, at * 2 + c))
-
-    def share_from(d):
-        at = y_at(d)
-        return copy(share_out.at[at], share_in.at[at], share_s.at[d], share_r.at[at], (g, at * 2 + c))
-
-    turns = sorted(range(1, ny), key=lambda d: -min(d, ny - d)) + [0]
-    pair_out[...] = share(1 - c).astype(BF16)
-    for d in turns:
-        pair_copy(d).start()
-    mine[...] = share(c)
-    for d in turns:
-        at = y_at(d)
-        pair_copy(d).wait_recv()
-        total = mine[at] + pair_in[at].astype(F32)
-        if d:
-            share_out[at] = total.astype(BF16)
-            share_to(d).start()
-    for d in turns[:-1]:
-        share_from(d).wait_recv()
-        total = total + share_in[y_at(d)].astype(F32)
-    incr_out[...] = total.reshape(nz, ROWS, width)
-
-    def incr_to(d):
-        at = z_at(d)
-        return copy(incr_out.at[at], final.at[z], incr_s.at[d], incr_r.at[z], in_z(at))
+        span = pl.ds(h * fore, fore)
+        return copy(share_out.at[d, span], share_in.at[at, span], share_s.at[d, h], share_r.at[at, h], (g, at * 2 + c))
+
+    def incr_to(t):
+        at = z_at(turns_z[t])
+        return copy(incr_out.at[t], final.at[z], incr_s.at[t], incr_r.at[z], in_z(at))
 
     def incr_from(d):
         at = z_at(d)
-        return copy(incr_out.at[at], final.at[at], incr_s.at[d], incr_r.at[at], in_z(at))
-
-    each(nz, lambda d: incr_to(d).start())
-    final[z] = incr_out[z]
+        return copy(incr_out.at[0], final.at[at], incr_s.at[0], incr_r.at[at], in_z(at))
+
+    for d in turns:
+        pair_out[d] = share(1 - c, d).astype(BF16)
+        pair_copy(d).start()
+    for d in turns:
+        total = share(c, d)
+        pair_copy(d).wait_recv()
+        total = total + pair_in[d].astype(F32)
+        if d:
+            share_out[d] = total.astype(BF16)
+            share_to(d, 0).start()
+    for d in turns[:-1]:
+        share_to(d, 1).start()
+    for h in range(2):
+        part = total[h * fore : (h + 1) * fore]
+        for d in turns[:-1]:
+            share_from(d, h).wait_recv()
+            part = part + share_in[y_at(d), h * fore : (h + 1) * fore].astype(F32)
+        for t in range(h * nz // 2, (h + 1) * nz // 2):
+            first = t * ROWS - h * fore
+            incr_out[t] = part[first : first + ROWS]
+            if t < nz - 1:
+                incr_to(t).start()
+    final[z] = incr_out[nz - 1]
     each(nz, lambda d: incr_from(d).wait_recv())
     for k in range(nz):
         at = slice(k * width, (k + 1) * width)
         out[:, at] = members[:, at].astype(F32) + final[k]
 
-    def obs_sent(d):
-        rows_to(d).wait_send()
-
     def y_sent(d):
         slab_to(d).wait_send()
         slab_pass(d).wait_send()
-        share_to(d).wait_send()
+        share_to(d, 0).wait_send()
+        share_to(d, 1).wait_send()
         pair_copy(d).wait_send()
 
     def z_sent(d):
         block_to(d).wait_send()
         pert_to(d).wait_send()
         pred_to(d).wait_send()
-        incr_to(d).wait_send()
 
     def x_sent(d):
         gram_to(d).wait_send()
         cross_to(d).wait_send()
         crosses_to(d).wait_send()
 
+    each(no, lambda d: rows_to(d).wait_send())
     half_copy.wait_send()
     slab_own.wait_send()
     pair_copy(0).wait_send()
-    each(no, obs_sent)
     each(ny, y_sent)
     each(nz, z_sent)
+    for t in range(nz - 1):
+        incr_to(t).wait_send()
     each(NX, x_sent)
 
 
@@ -497,7 +542,6 @@
     side, width = nz * ROWS, coeffs // nz
     vmem, many = pltpu.VMEM, pltpu.SemaphoreType.DMA
     signal = pltpu.SemaphoreType.REGULAR
-    stages = nz // 2 - 1
     return pl.pallas_call(
         lambda *refs: kernel(nm, no, *refs),
         out_shape=jax.ShapeDtypeStruct((ROWS, coeffs), F32),
@@ -519,7 +563,7 @@
             vmem((no, side, width), BF16),
             vmem((nz, no * ROWS, TILE), BF16),
             vmem((nz, no * ROWS, TILE), BF16),
-            vmem((NX, TILE + ROWS, TILE), F32),
+            vmem((NX, TILE // 2 + 2 * ROWS, TILE), F32),
             vmem((2, dims, 3, TILE, TILE), F32),
             vmem((4 * TILE, coeffs // 4), BF16),
             vmem((2, ny, side, TILE), F32),
@@ -527,7 +571,6 @@
             vmem((NX, TILE + ROWS, SLAB), F32),
             vmem((NX, TILE + ROWS, SLAB), F32),
             vmem((NX, TILE, SLAB), F32),
-            vmem((ny, side, width), F32),
             vmem((ny, side, width), BF16),
             vmem((ny, side, width), BF16),
             vmem((ny, side, width), BF16),
@@ -536,8 +579,7 @@
             vmem((nz, ROWS, width), F32),
             vmem((TILE, TILE), F32),
             vmem((TILE, TILE), F32),
-            signal((stages,)),
-            signal((stages,)),
+            signal,
             many((7,)),
             many((no,)),
             many((no,)),
@@ -559,8 +601,8 @@
             many((NX,)),
             many((ny,)),
             many((ny,)),
-            many((ny,)),
-            many((ny,)),
+            many((ny, 2)),
+            many((ny, 2)),
             many((nz,)),
             many((nz,)),
         ],

time: 54 us -> 48.7 us (0.902)
  Pallas kernels: 52.3 us -> 47 us
    pallas_call x1, Pallas kernels: 52.3 us -> 47 us  [shards(): pl.pallas_call(lambda *refs: kernel(nm, no, *refs), out_shape=jax.ShapeDt...]
where the time goes in v4:
time: 48.7 us; the launch traced here: 48.6 us
  Pallas kernels  47 us (97%)
  local copies, waits for them, and re-layouts  1.57 us (3%)
    pallas_call x1, Pallas kernels, shards(): pl.pallas_call(lambda *refs: kernel(nm, no, *refs), out_shape=jax.ShapeDt...  47 us
    unnamed x1, local copies, waits for them, and re-layouts  1.57 us

profile of v4, /device:TPU:1, one launch (start us, length us, event | category | flops | bytes accessed | tf_op | source)
XLA Modules:
  0.0 48.6 jit_solution(2266651501982172439)
XLA Ops:
  0.0 47.0 %shard_map.73 = f32[8,4096]{1,0:T(8,128)} custom-call(bf16[8,4096]{1,0:T(8,128)(2,1)} %refs_0_.1, s32[8,4096]{1,0:T(8,128)} %refs_1_.1, f32[8,1024]{1,0:T(8,128)} %refs_2_.1, s32[1,128]{1,0:T(1,128)} %bitcast.3, f32[1,128]{1,0:T(1,128)} %bitcast.4, f32[1,128]{1,0:T(1,128)} %bitcast.5, bf16[64,128]{1,0:T(8,128)(2,1)} %refs_6_.1), custom_call_target="tpu_custom_call" | custom-call | tf_op jit(solution)/shard_map/pallas_call | solution.py:545
  47.0 1.6 %copy.9 = f32[8,4096]{1,0:T(8,128)} copy(f32[8,4096]{1,0:T(8,128)} %shard_map.73) | data formatting | bytes 262144

commit v5 on v4

--- a/solution.py
+++ b/solution.py
@@ -414,7 +414,7 @@
     gram = unfolded(gram[: TILE // 2], gram[TILE // 2 + ROWS :])
     system = (gram - ensemble * mean_turned * mean_pred) * coupled[...] + spread[...]
 
-    inverted = inverse_blocks(system, 0, TILE // PANEL // 2)
+    inverted = inverse_blocks(system, 0, TILE // PANEL // 4)
 
     each(NX, lambda d: cross_from(d).wait_recv())
     cross = cross_in[0]
@@ -440,7 +440,7 @@
         for k in range(no):
             innov[k % 2, k // 2, t * ROWS : (t + 1) * ROWS, :] = left[k * ROWS : (k + 1) * ROWS]
 
-    inverted = inverse_blocks(inverted, TILE // PANEL // 2, TILE // PANEL)
+    inverted = inverse_blocks(inverted, TILE // PANEL // 4, TILE // PANEL)
 
     each(NX, lambda d: crosses_from(d).wait_recv())
     cross = jnp.concatenate([crosses[k] for k in range(NX)], axis=1)
@@ -481,10 +481,10 @@
     for d in turns:
         pair_out[d] = share(1 - c, d).astype(BF16)
         pair_copy(d).start()
+    mine = {d: share(c, d) for d in turns}
     for d in turns:
-        total = share(c, d)
         pair_copy(d).wait_recv()
-        total = total + pair_in[d].astype(F32)
+        total = mine[d] + pair_in[d].astype(F32)
         if d:
             share_out[d] = total.astype(BF16)
             share_to(d, 0).start()

time: 48.7 us -> 48.1 us (0.988)
  Pallas kernels: 47 us -> 46 us
    pallas_call x1, Pallas kernels: 47 us -> 46 us  [shards(): pl.pallas_call(lambda *refs: kernel(nm, no, *refs), out_shape=jax.ShapeDt...]
where the time goes in v5:
time: 48.1 us; the launch traced here: 47.6 us
  Pallas kernels  46 us (96%)
  local copies, waits for them, and re-layouts  1.57 us (3%)
    pallas_call x1, Pallas kernels, shards(): pl.pallas_call(lambda *refs: kernel(nm, no, *refs), out_shape=jax.ShapeDt...  46 us
    unnamed x1, local copies, waits for them, and re-layouts  1.57 us

profile of v5, /device:TPU:1, one launch (start us, length us, event | category | flops | bytes accessed | tf_op | source)
XLA Modules:
  0.0 47.6 jit_solution(18000945060591696388)
XLA Ops:
  0.0 46.0 %shard_map.73 = f32[8,4096]{1,0:T(8,128)} custom-call(bf16[8,4096]{1,0:T(8,128)(2,1)} %refs_0_.1, s32[8,4096]{1,0:T(8,128)} %refs_1_.1, f32[8,1024]{1,0:T(8,128)} %refs_2_.1, s32[1,128]{1,0:T(1,128)} %bitcast.3, f32[1,128]{1,0:T(1,128)} %bitcast.4, f32[1,128]{1,0:T(1,128)} %bitcast.5, bf16[64,128]{1,0:T(8,128)(2,1)} %refs_6_.1), custom_call_target="tpu_custom_call" | custom-call | tf_op jit(solution)/shard_map/pallas_call | solution.py:545
  46.0 1.6 %copy.9 = f32[8,4096]{1,0:T(8,128)} copy(f32[8,4096]{1,0:T(8,128)} %shard_map.73) | data formatting | bytes 262144

commit v6 on v5

--- a/solution.py
+++ b/solution.py
@@ -375,7 +375,8 @@
         at = x_at(d)
         return copy(grams.at[at], grams.at[at], grams_s.at[d], grams_r.at[at], in_x(at))
 
-    each(NX, lambda d: gram_to(d).start())
+    for d in sorted(range(1, NX), key=lambda d: -min(d, NX - d)):
+        gram_to(d).start()
     for d in far:
         pert_to(d).start()
 
@@ -391,19 +392,24 @@
     raw = dot(ordered, slab, FIRST)
     total = dot(ones, slab, PLAIN)[:ROWS]
     for k in range(NX):
-        cross_out[k, :TILE] = raw[:, k * SLAB : (k + 1) * SLAB]
-        cross_out[k, TILE:] = total[:, k * SLAB : (k + 1) * SLAB]
+        cross_out[k, :ROWS] = total[:, k * SLAB : (k + 1) * SLAB]
+        cross_out[k, ROWS:] = raw[:, k * SLAB : (k + 1) * SLAB]
     cross_in[x] = cross_out[x]
 
-    def cross_to(d):
+    def piece(h):
+        return pl.ds(h * (TILE // 2 + ROWS), TILE // 2 + ROWS * (1 - h))
+
+    def cross_to(d, h):
         at = x_at(d)
-        return copy(cross_out.at[at], cross_in.at[x], cross_s.at[d], cross_r.at[x], in_x(at))
-
-    def cross_from(d):
+        return copy(cross_out.at[at, piece(h)], cross_in.at[x, piece(h)], cross_s.at[d, h], cross_r.at[x, h], in_x(at))
+
+    def cross_from(d, h):
         at = x_at(d)
-        return copy(cross_out.at[at], cross_in.at[at], cross_s.at[d], cross_r.at[at], in_x(at))
-
-    each(NX, lambda d: cross_to(d).start())
+        return copy(cross_out.at[at, piece(h)], cross_in.at[at, piece(h)], cross_s.at[d, h], cross_r.at[at, h], in_x(at))
+
+    for h in range(2):
+        for d in sorted(range(1, NX), key=lambda d: -min(d, NX - d)):
+            cross_to(d, h).start()
 
     each(NX, lambda d: gram_from(d).wait_recv())
     gram = grams[0]
@@ -416,21 +422,31 @@
 
     inverted = inverse_blocks(system, 0, TILE // PANEL // 4)
 
-    each(NX, lambda d: cross_from(d).wait_recv())
-    cross = cross_in[0]
-    for k in range(1, NX):
-        cross = cross + cross_in[k]
-    mean_param = cross[TILE : TILE + 1] / ensemble
-    crosses[x] = cross[:TILE] - ensemble * mean_turned * mean_param
-
-    def crosses_to(d):
-        return copy(crosses.at[x], crosses.at[x], crosses_s.at[d], crosses_r.at[x], in_x(x_at(d)))
-
-    def crosses_from(d):
+    def crosses_to(d, h):
+        span = crosses.at[x, pl.ds(h * TILE // 2, TILE // 2)]
+        return copy(span, span, crosses_s.at[d, h], crosses_r.at[x, h], in_x(x_at(d)))
+
+    def crosses_from(d, h):
         at = x_at(d)
-        return copy(crosses.at[at], crosses.at[at], crosses_s.at[d], crosses_r.at[at], in_x(at))
-
-    each(NX, lambda d: crosses_to(d).start())
+        span = crosses.at[at, pl.ds(h * TILE // 2, TILE // 2)]
+        return copy(span, span, crosses_s.at[d, h], crosses_r.at[at, h], in_x(at))
+
+    mean_param = None
+    for h in range(2):
+        for d in range(1, NX):
+            cross_from(d, h).wait_recv()
+        cross = cross_in[0, piece(h)]
+        for k in range(1, NX):
+            cross = cross + cross_in[k, piece(h)]
+        if h == 0:
+            mean_param = cross[:1] / ensemble
+            cross = cross[ROWS:]
+        part = slice(h * TILE // 2, (h + 1) * TILE // 2)
+        crosses[x, part] = cross - ensemble * mean_turned[part] * mean_param
+        for d in sorted(range(1, NX), key=lambda d: -min(d, NX - d)):
+            crosses_to(d, h).start()
+        if h == 0:
+            inverted = inverse_blocks(inverted, TILE // PANEL // 4, TILE // PANEL // 2)
 
     each(nz, lambda d: pert_from(d).wait_recv())
     noise_root = jnp.sqrt(noise[...])
@@ -440,9 +456,11 @@
         for k in range(no):
             innov[k % 2, k // 2, t * ROWS : (t + 1) * ROWS, :] = left[k * ROWS : (k + 1) * ROWS]
 
-    inverted = inverse_blocks(inverted, TILE // PANEL // 4, TILE // PANEL)
-
-    each(NX, lambda d: crosses_from(d).wait_recv())
+    inverted = inverse_blocks(inverted, TILE // PANEL // 2, TILE // PANEL)
+
+    for h in range(2):
+        for d in range(1, NX):
+            crosses_from(d, h).wait_recv()
     cross = jnp.concatenate([crosses[k] for k in range(NX)], axis=1)
     gain = dot(inverted, cross, PLAIN, lax.Precision.HIGHEST) / (ensemble - 1)
     high = gain.astype(BF16)
@@ -501,11 +519,6 @@
             if t < nz - 1:
                 incr_to(t).start()
     final[z] = incr_out[nz - 1]
-    each(nz, lambda d: incr_from(d).wait_recv())
-    for k in range(nz):
-        at = slice(k * width, (k + 1) * width)
-        out[:, at] = members[:, at].astype(F32) + final[k]
-
     def y_sent(d):
         slab_to(d).wait_send()
         slab_pass(d).wait_send()
@@ -520,8 +533,9 @@
 
     def x_sent(d):
         gram_to(d).wait_send()
-        cross_to(d).wait_send()
-        crosses_to(d).wait_send()
+        for h in range(2):
+            cross_to(d, h).wait_send()
+            crosses_to(d, h).wait_send()
 
     each(no, lambda d: rows_to(d).wait_send())
     half_copy.wait_send()
@@ -529,6 +543,13 @@
     pair_copy(0).wait_send()
     each(ny, y_sent)
     each(nz, z_sent)
+    for d in reversed(turns_z):
+        at = z_at(d)
+        if d:
+            incr_from(d).wait_recv()
+        place = pl.ds(pl.multiple_of(at * width, width), width)
+        out[:, place] = members[:, place].astype(F32) + final[at]
+
     for t in range(nz - 1):
         incr_to(t).wait_send()
     each(NX, x_sent)
@@ -595,10 +616,10 @@
             many((nz,)),
             many((NX,)),
             many((NX,)),
-            many((NX,)),
-            many((NX,)),
-            many((NX,)),
-            many((NX,)),
+            many((NX, 2)),
+            many((NX, 2)),
+            many((NX, 2)),
+            many((NX, 2)),
             many((ny,)),
             many((ny,)),
             many((ny, 2)),

time: 48.1 us -> 46.5 us (0.967)
  Pallas kernels: 46 us -> 44.7 us
    pallas_call x1, Pallas kernels: 46 us -> 44.7 us  [shards(): pl.pallas_call(lambda *refs: kernel(nm, no, *refs), out_shape=jax.ShapeDt...]
where the time goes in v6:
time: 46.5 us; the launch traced here: 46.3 us
  Pallas kernels  44.7 us (96%)
  local copies, waits for them, and re-layouts  1.57 us (3%)
    pallas_call x1, Pallas kernels, shards(): pl.pallas_call(lambda *refs: kernel(nm, no, *refs), out_shape=jax.ShapeDt...  44.7 us
    unnamed x1, local copies, waits for them, and re-layouts  1.57 us

profile of v6, /device:TPU:1, one launch (start us, length us, event | category | flops | bytes accessed | tf_op | source)
XLA Modules:
  0.0 46.3 jit_solution(14798196560731710717)
XLA Ops:
  0.0 44.7 %shard_map.73 = f32[8,4096]{1,0:T(8,128)} custom-call(bf16[8,4096]{1,0:T(8,128)(2,1)} %refs_0_.1, s32[8,4096]{1,0:T(8,128)} %refs_1_.1, f32[8,1024]{1,0:T(8,128)} %refs_2_.1, s32[1,128]{1,0:T(1,128)} %bitcast.3, f32[1,128]{1,0:T(1,128)} %bitcast.4, f32[1,128]{1,0:T(1,128)} %bitcast.5, bf16[64,128]{1,0:T(8,128)(2,1)} %refs_6_.1), custom_call_target="tpu_custom_call" | custom-call | tf_op jit(solution)/shard_map/pallas_call | solution.py:566
  44.7 1.6 %copy.9 = f32[8,4096]{1,0:T(8,128)} copy(f32[8,4096]{1,0:T(8,128)} %shard_map.73) | data formatting | bytes 262144

commit v7 on v6

--- a/solution.py
+++ b/solution.py
@@ -352,15 +352,17 @@
         return copy(slabs.at[at], slabs.at[at], slabs_s.at[ny + d], slabs_r.at[at], (g, sibling))
 
     slab_own = copy(slabs.at[o], slabs.at[o], slabs_s.at[0], slabs_r.at[o], (g, sibling))
-    each(ny, lambda d: slab_to(d).start())
     slab_own.start()
+    for d in turns[:-1]:
+        slab_to(d).start()
 
     def pass_on(d):
         at = y_at(d) * 2 + c
         slab_from(at, at).wait_recv()
         slab_pass(d).start()
 
-    each(ny, pass_on)
+    for d in reversed(turns[:-1]):
+        pass_on(d)
 
     each(nz, lambda d: pred_from(d).wait_recv())
     flat = preds[...].reshape(line, TILE)

time: 46.5 us -> 47.1 us (1.013)
  Pallas kernels: 44.7 us -> 45.5 us
    pallas_call x1, Pallas kernels: 44.7 us -> 45.5 us  [shards(): pl.pallas_call(lambda *refs: kernel(nm, no, *refs), out_shape=jax.ShapeDt...]
where the time goes in v7:
time: 47.1 us; the launch traced here: 47 us
  Pallas kernels  45.5 us (97%)
  local copies, waits for them, and re-layouts  1.57 us (3%)
    pallas_call x1, Pallas kernels, shards(): pl.pallas_call(lambda *refs: kernel(nm, no, *refs), out_shape=jax.ShapeDt...  45.5 us
    unnamed x1, local copies, waits for them, and re-layouts  1.57 us

profile of v7, /device:TPU:1, one launch (start us, length us, event | category | flops | bytes accessed | tf_op | source)
XLA Modules:
  0.0 47.0 jit_solution(15855252671849386863)
XLA Ops:
  0.0 45.5 %shard_map.73 = f32[8,4096]{1,0:T(8,128)} custom-call(bf16[8,4096]{1,0:T(8,128)(2,1)} %refs_0_.1, s32[8,4096]{1,0:T(8,128)} %refs_1_.1, f32[8,1024]{1,0:T(8,128)} %refs_2_.1, s32[1,128]{1,0:T(1,128)} %bitcast.3, f32[1,128]{1,0:T(1,128)} %bitcast.4, f32[1,128]{1,0:T(1,128)} %bitcast.5, bf16[64,128]{1,0:T(8,128)(2,1)} %refs_6_.1), custom_call_target="tpu_custom_call" | custom-call | tf_op jit(solution)/shard_map/pallas_call | solution.py:568
  45.5 1.6 %copy.9 = f32[8,4096]{1,0:T(8,128)} copy(f32[8,4096]{1,0:T(8,128)} %shard_map.73) | data formatting | bytes 262144
